TPU v7x, 32 devices: a whole 2x2x4 slice. The times are simulated.
32 devices in a mesh: row: 8 (over y, x, core), col: 4 (over z).
Axes of the slice: x: 2, y: 2, z: 4, core: 2. Of those that a mesh axis runs over, the one named last changes fastest.
Arguments:
- inputs: bfloat16 [768, 12288], P(None, 'col'), may hold values from -6 to 6
- out_grad: bfloat16 [768, 12288], P(None, 'col'), may hold values from -6 to 6
- pre_act: bfloat16 [768, 24576], P('col', 'row'), may hold values from -8 to 8
- w_in: bfloat16 [12288, 24576], P('col', 'row'), may hold values from -0.0546875 to 0.0546875
- w_out: bfloat16 [24576, 12288], P('row', 'col'), may hold values from -0.0390625 to 0.0390625
Outputs:
- grad_inputs: bfloat16 [768, 12288], P('row', 'col')
- grad_w_in: bfloat16 [12288, 24576], P('col', 'row')
- grad_w_out: bfloat16 [24576, 12288], P('row', 'col')
All inputs are finite; a program needn't handle non-finite values.
Results may differ from a plain program's by a relative error of at most 0.0049.
Values may be sent and summed in bfloat16 or wider, within the bound.
No kernel may reach another device: no remote copies, remote signals or barrier semaphores. Data moves between devices by JAX's collectives and lax.ppermute only.
A program may use at most 192 MiB of HBM per device.

v0:
```python
import math

import jax
import jax.numpy as jnp
from jax import lax
from jax.sharding import PartitionSpec as P

coef_c = math.sqrt(2.0 / math.pi)


def gelu_parts(pre_values):
    hval = pre_values.astype(jnp.float32)
    tval = jnp.tanh(coef_c * (hval + 0.044715 * hval * hval * hval))
    activ = 0.5 * hval * (1.0 + tval)
    deriv = 0.5 * (1.0 + tval) + 0.5 * hval * (1.0 - tval * tval) * coef_c * (
        1.0 + 3.0 * 0.044715 * hval * hval
    )
    return (activ, deriv)


def per_device(inputs, out_grad, pre_act, w_in, w_out):
    total_tokens = inputs.shape[0]
    scale_value = 1.0 / math.sqrt(total_tokens)
    block = out_grad
    act_share = lax.psum_scatter(
        lax.dot_general(block, w_out, (((1,), (1,)), ((), ())), preferred_element_type=jnp.float32),
        "col",
        scatter_dimension=0,
        tiled=True,
    )
    local_act, local_deriv = gelu_parts(pre_act)
    hid_share = (act_share * local_deriv).astype(jnp.bfloat16)
    activ_all, hid_all = (
        lax.all_gather(local_act.astype(jnp.bfloat16), "col", axis=0, tiled=True),
        lax.all_gather(hid_share, "col", axis=0, tiled=True),
    )
    grad_w_out = lax.dot_general(
        activ_all, out_grad, (((0,), (0,)), ((), ())), preferred_element_type=jnp.float32
    )
    grad_w_out = (grad_w_out * scale_value).astype(jnp.bfloat16)
    grad_w_in = lax.dot_general(
        inputs, hid_all, (((0,), (0,)), ((), ())), preferred_element_type=jnp.float32
    )
    grad_w_in = (grad_w_in * scale_value).astype(jnp.bfloat16)
    block = hid_all
    grad_inputs = lax.psum_scatter(
        lax.dot_general(block, w_in, (((1,), (1,)), ((), ())), preferred_element_type=jnp.float32),
        "row",
        scatter_dimension=0,
        tiled=True,
    )
    return (grad_inputs.astype(jnp.bfloat16), grad_w_in, grad_w_out)


def solution(mesh):
    placed = (P(None, "col"), P(None, "col"), P("col", "row"), P("col", "row"), P("row", "col"))
    return jax.shard_map(
        per_device,
        mesh=mesh,
        in_specs=placed,
        out_specs=(P("row", "col"), P("col", "row"), P("row", "col")),
        check_vma=False,
    )
```

profile of v0, /device:TPU:0, one launch (start us, length us, event | category | flops | bytes accessed | tf_op | source)
XLA Modules:
  0.0 464.1 jit_solution(5129909337847586142)
XLA Ops:
  7.2 0.0 reduce-scatter.3.cloned.1.call-start
  7.2 21.1 %fusion.12 = f32[768,3072]{1,0:T(8,128)} fusion(bf16[768,3072]{1,0:T(8,128)(2,1)} %param.6, bf16[3072,3072]{1,0:T(8,128)(2,1)} %param.9), kind=kOutput, calls=%fused_computation.21 | convolution fusion | flops 14495514624 | bytes 33030144 | tf_op jit(solution)/shard_map/dot_general | solution.py:26
  28.3 0.0 copy-start
  28.3 0.0 reduce-scatter.3.cloned.1.call-update
  28.3 0.0 all-gather.3.cloned.1.call-start
  28.3 164.1 %reduce-scatter.3.cloned.1.call-done = f32[192,3072]{1,0:T(8,128)} async-done(((f32[768,3072]{1,0:T(8,128)}), f32[192,3072]{1,0:T(8,128)}) %reduce-scatter.3.cloned.1.call-update) | async-done | bytes 2359312 | tf_op jit(solution)/shard_map/reduce_scatter | solution.py:25
  192.4 0.0 copy-done
  192.4 4.8 %fusion.8 = (bf16[192,3072]{1,0:T(8,128)(2,1)}, bf16[192,3072]{1,0:T(8,128)(2,1)}) fusion(bf16[192,3072]{1,0:T(8,128)(2,1)S(1)} %copy-done, f32[192,3072]{1,0:T(8,128)} %reduce-scatter.3.cloned.1.call-done), kind=kLoop, calls=%fused_computation.17 | loop fusion | flops 12976128 | bytes 5898240 | tf_op jit(solution)/shard_map/convert_element_type | solution.py:34
  197.2 0.0 all-gather.3.cloned.1.call-update
  197.2 0.0 all-gather.5.cloned.1.call-start
  197.2 0.7 all-gather.5.cloned.1.call-update
  197.9 0.2 reduce-scatter.5.cloned.1.call-start
  198.2 89.4 %all-gather.3.cloned.1.call-done = bf16[768,3072]{1,0:T(8,128)(2,1)} async-done(((bf16[192,3072]{1,0:T(8,128)(2,1)}), bf16[768,3072]{1,0:T(8,128)(2,1)}) %all-gather.3.cloned.1.call-update) | async-done | bytes 4718608 | tf_op jit(solution)/shard_map/all_gather | solution.py:35
  287.6 21.1 %fusion.13 = f32[768,3072]{1,0:T(8,128)} fusion(bf16[768,3072]{1,0:T(8,128)(2,1)} %all-gather.3.cloned.1.call-done, bf16[3072,3072]{1,0:T(8,128)(2,1)} %param.8), kind=kOutput, calls=%fused_computation.22 | convolution fusion | flops 14495514624 | bytes 33030144 | tf_op jit(solution)/shard_map/dot_general | solution.py:47
  308.7 0.0 reduce-scatter.5.cloned.1.call-update
  308.7 21.0 %fusion = bf16[3072,3072]{0,1:T(8,128)(2,1)} fusion(bf16[768,3072]{1,0:T(8,128)(2,1)} %all-gather.3.cloned.1.call-done, bf16[768,3072]{1,0:T(8,128)(2,1)} %param.5), kind=kOutput, calls=%fused_computation.2 | convolution fusion | flops 14514388992 | bytes 28311552 | tf_op jit(solution)/shard_map/dot_general | solution.py:41
  329.8 24.6 %copy.8 = bf16[3072,3072]{1,0:T(8,128)(2,1)} copy(bf16[3072,3072]{0,1:T(8,128)(2,1)} %fusion) | data formatting | bytes 37748736
  354.4 22.7 %all-gather.5.cloned.1.call-done = bf16[768,3072]{1,0:T(8,128)(2,1)} async-done(((bf16[192,3072]{1,0:T(8,128)(2,1)}), bf16[768,3072]{1,0:T(8,128)(2,1)}) %all-gather.5.cloned.1.call-update) | async-done | bytes 4718608 | tf_op jit(solution)/shard_map/all_gather | solution.py:34
  377.1 21.0 %multiply_convert_fusion = bf16[3072,3072]{1,0:T(8,128)(2,1)} fusion(bf16[768,3072]{1,0:T(8,128)(2,1)} %all-gather.5.cloned.1.call-done, bf16[768,3072]{1,0:T(8,128)(2,1)} %param.6), kind=kOutput, calls=%fused_computation | convolution fusion | flops 14514388992 | bytes 28311552 | tf_op jit(solution)/shard_map/dot_general | solution.py:37
  398.1 57.4 %reduce-scatter.5.cloned.1.call-done = f32[96,3072]{1,0:T(8,128)} async-done(((f32[768,3072]{1,0:T(8,128)}), f32[96,3072]{1,0:T(8,128)}) %reduce-scatter.5.cloned.1.call-update) | async-done | bytes 1179664 | tf_op jit(solution)/shard_map/reduce_scatter | solution.py:46
  455.4 2.2 convert_element_type.23
Async XLA Ops:
  7.2 185.3 %reduce-scatter.3.cloned.1.call-start = ((), (), s32[]{:S(2)}) async-start(), calls=%async_computation.2 | async-start | bytes 11796480 | tf_op jit(solution)/shard_map/reduce_scatter | solution.py:25
  28.3 164.2 %copy-start = (bf16[192,3072]{1,0:T(8,128)(2,1)S(1)}, bf16[192,3072]{1,0:T(8,128)(2,1)}, u32[]{:S(2)}) copy-start(bf16[192,3072]{1,0:T(8,128)(2,1)} %param.7) | copy-start | bytes 3538948
  28.3 259.3 %all-gather.3.cloned.1.call-start = ((), (), s32[]{:S(2)}) async-start(), calls=%async_computation.3 | async-start | bytes 5898240 | tf_op jit(solution)/shard_map/all_gather | solution.py:35
  197.2 179.9 %all-gather.5.cloned.1.call-start = ((), (), s32[]{:S(2)}) async-start(), calls=%async_computation.5 | async-start | bytes 5898240 | tf_op jit(solution)/shard_map/all_gather | solution.py:34
  197.9 257.5 %reduce-scatter.5.cloned.1.call-start = ((), (), s32[]{:S(2)}) async-start(), calls=%async_computation.4 | async-start | bytes 10616832 | tf_op jit(solution)/shard_map/reduce_scatter | solution.py:46
Sparse Core Ops, SparseCore 0:
  28.4 163.9 reduce-scatter.2
  197.3 90.2 all-gather.2
  289.2 87.8 all-gather.4
  380.4 74.9 reduce-scatter.4
where the time goes:
time: 465 us; the launch traced here: 464 us
  waiting for transfers between devices  334 us (72%)
  matrix products  84.2 us (18%)
  local copies, waits for them, and re-layouts  24.6 us (5%)
  between operations  13.8 us (3%)
  other arithmetic  6.9 us (1%)
    reduce_scatter x1, waiting for transfers between devices, per_device(): lax.psum_scatter(lax.dot_general(block, w_out, (((1,), (1,)), ((), ())),...  164 us
    all_gather x1, waiting for transfers between devices, per_device(): lax.all_gather(hid_share, 'col', axis=0, tiled=True)  89.4 us
    reduce_scatter x1, waiting for transfers between devices, per_device(): lax.psum_scatter(lax.dot_general(block, w_in, (((1,), (1,)), ((), ())), p...  57.4 us
    unnamed x3, local copies, waits for them, and re-layouts  24.6 us
    all_gather x1, waiting for transfers between devices, per_device(): lax.all_gather(local_act.astype(jnp.bfloat16), 'col', axis=0, tiled=True)  22.7 us
    dot_general x1, matrix products, per_device(): lax.dot_general(block, w_in, (((1,), (1,)), ((), ())), preferred_element_...  21.1 us
    dot_general x1, matrix products, per_device(): lax.dot_general(block, w_out, (((1,), (1,)), ((), ())), preferred_element...  21.1 us
    dot_general x1, matrix products, per_device(): lax.dot_general(inputs, hid_all, (((0,), (0,)), ((), ())), preferred_elem...  21 us
  transfers between devices with their start and end apart: 4, of which 4 were waited for; matrix products, arithmetic and copies ran while one was open for 19% of the time, Pallas kernels for 0%

commit v1 on v0

v1 whole, which is shorter than its diff:
```python
import functools
import math

import jax
import jax.numpy as jnp
from jax import lax
from jax.experimental import pallas as pl
from jax.experimental.pallas import tpu as pltpu
from jax.sharding import PartitionSpec as P

coef_c = math.sqrt(2.0 / math.pi)
SMALL, LARGE = 26 * 1024 * 1024, 44 * 1024 * 1024
NT = (((1,), (1,)), ((), ()))
NN = (((1,), (0,)), ((), ()))


def gelu_parts(pre_values):
    hval = pre_values.astype(jnp.float32)
    tval = jnp.tanh(coef_c * (hval + 0.044715 * hval * hval * hval))
    activ = 0.5 * hval * (1.0 + tval)
    deriv = 0.5 * (1.0 + tval) + 0.5 * hval * (1.0 - tval * tval) * coef_c * (
        1.0 + 3.0 * 0.044715 * hval * hval
    )
    return (activ, deriv)


def dot32(a, b, dims):
    return lax.dot_general(a, b, dims, preferred_element_type=jnp.float32)


ANY = pl.BlockSpec(memory_space=pl.ANY)
TN = (((0,), (0,)), ((), ()))
TOKEN = jax.ShapeDtypeStruct((8, 128), jnp.float32)
SIDE, PLACE, OUTER, CORE, X, Y = range(6)


def call(body, place, steps, in_specs, out_specs, out_shapes, operands, after, scratch=(), aliases=None, vmem=SMALL):
    n_in, n_out = len(operands), len(out_shapes)

    def kernel(place_ref, *refs):
        outs = refs[n_in + 1:n_in + 1 + n_out]
        refs[n_in + 1 + n_out][...] = jnp.zeros((8, 128), jnp.float32)
        body(place_ref, *refs[:n_in], *outs, *refs[n_in + 2 + n_out:])

    return pl.pallas_call(
        kernel,
        grid_spec=pltpu.PrefetchScalarGridSpec(
            num_scalar_prefetch=1,
            grid=(steps,),
            in_specs=list(in_specs) + [ANY],
            out_specs=list(out_specs) + [pl.BlockSpec((8, 128), lambda i, s: (0, 0))],
            scratch_shapes=list(scratch),
        ),
        out_shape=list(out_shapes) + [TOKEN],
        input_output_aliases=aliases or {},
        compiler_params=pltpu.CompilerParams(vmem_limit_bytes=vmem, dimension_semantics=("arbitrary",)),
        cost_estimate=pl.CostEstimate(flops=0, bytes_accessed=0, transcendentals=0),
    )(place, *operands, after)


def shape16(*sizes):
    return jax.ShapeDtypeStruct(sizes, jnp.bfloat16)


def shape32(*sizes):
    return jax.ShapeDtypeStruct(sizes, jnp.float32)


def whole(*sizes):
    return pl.BlockSpec(sizes, lambda i, s: (0,) * len(sizes))


def choose(place_ref, which, put, ones, zeros):
    pl.when(place_ref[which] == 1)(lambda: put(ones))
    pl.when(place_ref[which] == 0)(lambda: put(zeros))


def act_partial(place, out_grad, w_out, start, width, after):
    tokens, model = out_grad.shape
    bw = 256

    def body(place_ref, grad, w, out):
        out[...] = dot32(grad[...], w[...], NT).astype(out.dtype)

    return call(
        body, place, width // bw,
        [whole(tokens, model), pl.BlockSpec((bw, model), lambda i, s: (start // bw + i, 0))],
        [pl.BlockSpec((tokens, bw), lambda i, s: (0, i))],
        [shape16(tokens, width)], (out_grad, w_out), after, vmem=LARGE,
    )


def own_piece(place, pre_act, start, width, after):
    rows = pre_act.shape[0]

    def body(place_ref, pre, out):
        out[...] = pre[...]

    return call(
        body, place, 1, [pl.BlockSpec((rows, width), lambda i, s: (0, start // width))], [whole(rows, width)],
        [shape16(rows, width)], (pre_act,), after,
    )


def near_half(place, own, other, after):
    rows, width = own.shape
    cut = width // 2

    def body(place_ref, mine, theirs, out):
        def put(pair):
            for k in range(2):
                for n, ref in enumerate(pair):
                    out[(2 * k + n) * rows:(2 * k + n + 1) * rows, :] = ref[:, k * cut:(k + 1) * cut]

        choose(place_ref, PLACE, put, (theirs, mine), (mine, theirs))

    return call(
        body, place, 1, [whole(rows, width)] * 2, [whole(4 * rows, cut)], [shape16(4 * rows, cut)],
        (own, other), after,
    )


def gate(place, value, after):
    return call(
        lambda *refs: None, place, 1, [ANY], [ANY], [jax.ShapeDtypeStruct(value.shape, value.dtype)],
        (value,), after, aliases={1: 0},
    )


def either(place, outers, inners, after):
    rows, width = inners.shape
    block = pl.BlockSpec((rows // 2, width), lambda i, s: (i, 0))

    def body(place_ref, a, b, out):
        def put(ref):
            out[...] = ref[...]

        choose(place_ref, OUTER, put, a, b)

    return call(body, place, 2, [block, block], [block], [shape16(rows, width)], (outers, inners), after)


def add_partials(place, mine, got, after):
    tokens, width = mine.shape

    def body(place_ref, a, b, out):
        out[...] = (a[...].astype(jnp.float32) + b[...].astype(jnp.float32)).astype(out.dtype)

    block = pl.BlockSpec((tokens // 2, width), lambda i, s: (i, 0))
    return call(body, place, 2, [block, block], [block], [shape16(tokens, width)], (mine, got), after)


def hid_part(place, mine, got, crossed, near, far, half_of, outers, after):
    tokens, width = mine.shape
    half = tokens // 2

    def body(place_ref, a, b, c, near_ref, far_ref, *rest):
        out = rest[-1]

        @pl.when(place_ref[OUTER] == 1)
        def _():
            out[...] = rest[0][...] if len(rest) == 2 else jnp.zeros_like(out)

        def fill(pre):
            total = a[...].astype(jnp.float32) + b[...].astype(jnp.float32) + c[...].astype(jnp.float32)
            out[...] = (total * gelu_parts(pre[...])[1]).astype(out.dtype)

        inner = place_ref[OUTER] == 0
        here = pl.program_id(0) == place_ref[SIDE]
        pl.when(inner & here)(lambda: fill(near_ref))
        pl.when(inner & jnp.logical_not(here))(lambda: fill(far_ref))

    block = pl.BlockSpec((half, width), lambda i, s: (i, 0))
    pre = pl.BlockSpec((half, width), lambda i, s: (half_of, 0))
    operands = [mine, got, crossed, near, far] + ([] if outers is None else [outers])
    specs = [block, block, block, pre, pre] + ([] if outers is None else [block])
    return call(body, place, 2, specs, [block], [shape16(tokens, width)], operands, after)


def out_weight(place, near, cross, got, half_of, out_grad, start, total, scale, into, after):
    tokens, width = near.shape
    half, model = tokens // 2, out_grad.shape[1]
    bd = 1024

    def body(place_ref, near_ref, cross_ref, got_ref, og_near, og_far, *rest):
        out, activ = rest[-2:]

        @pl.when(pl.program_id(0) == 0)
        def _():
            def fill(ref, first):
                for c in range(0, half, 128):
                    value = gelu_parts(ref[c:c + 128, :])[0]
                    activ[first + c:first + c + 128, :] = value.astype(activ.dtype)

            fill(near_ref, 0)
            choose(place_ref, OUTER, lambda ref: fill(ref, half), got_ref, cross_ref)

        value = dot32(activ[:half], og_near[...], TN) + dot32(activ[half:], og_far[...], TN)
        out[...] = (value * scale).astype(out.dtype)

    operands = [near, cross, got, out_grad, out_grad]
    specs = [pl.BlockSpec((half, width), lambda i, s: (half_of, 0))] * 3 + [
        pl.BlockSpec((half, bd), lambda i, s: (s[SIDE], i)),
        pl.BlockSpec((half, bd), lambda i, s: (1 - s[SIDE], i)),
    ]
    aliases = None
    if into is not None:
        operands.append(into)
        specs.append(ANY)
        aliases = {6: 0}
    assert start % width == 0
    return call(
        body, place, model // bd, specs,
        [pl.BlockSpec((width, bd), lambda i, s: (start // width, i))],
        [shape16(total, model)], operands, after,
        scratch=[pltpu.VMEM((tokens, width), jnp.bfloat16)], aliases=aliases,
    )


def join(place_ref, refs, hid):
    def put(parts):
        column = 0
        for ref in parts:
            width = ref.shape[1]
            hid[:, column:column + width] = ref[...]
            column += width

    choose(place_ref, OUTER, put, refs[1::2], refs[0::2])


def in_weight(place, inputs, parts, start, total, scale, into, after):
    tokens, model = inputs.shape
    flat = [part for pair in parts for part in pair]
    width = sum(part.shape[1] for part in flat) // 2
    bd = 1024

    def body(place_ref, x, *rest):
        out, hid = rest[-2:]
        pl.when(pl.program_id(0) == 0)(lambda: join(place_ref, rest[:len(flat)], hid))
        out[...] = (dot32(x[...], hid[...], TN) * scale).astype(out.dtype)

    operands = [inputs] + flat
    specs = [pl.BlockSpec((tokens, bd), lambda i, s: (0, i))] + [whole(*part.shape) for part in flat]
    aliases = None
    if into is not None:
        aliases = {1 + len(operands): 0}
        operands.append(into)
        specs.append(ANY)
    assert start % width == 0
    return call(
        body, place, model // bd, specs,
        [pl.BlockSpec((bd, width), lambda i, s: (i, start // width))],
        [shape16(model, total)], operands, after,
        scratch=[pltpu.VMEM((tokens, width), jnp.bfloat16)], aliases=aliases,
    )


def in_partial(place, parts, w_in, start, after):
    model = w_in.shape[0]
    flat = [part for pair in parts for part in pair]
    tokens = flat[0].shape[0]
    width = sum(part.shape[1] for part in flat) // 2
    bd = 512

    def body(place_ref, w, *rest):
        out, hid = rest[-2:]
        pl.when(pl.program_id(0) == 0)(lambda: join(place_ref, rest[:len(flat)], hid))
        out[...] = dot32(hid[...], w[...], NT)

    assert start % width == 0
    return call(
        body, place, model // bd,
        [pl.BlockSpec((bd, width), lambda i, s: (i, start // width))] + [whole(*part.shape) for part in flat],
        [pl.BlockSpec((tokens, bd), lambda i, s: (0, i))],
        [shape32(tokens, model)], [w_in] + flat, after,
        scratch=[pltpu.VMEM((tokens, width), jnp.bfloat16)], vmem=LARGE,
    )


def in_last(place, parts, w_in, start, total, after):
    model = w_in.shape[0]
    flat = [part for pair in parts for part in pair]
    tokens = flat[0].shape[0]
    width = sum(part.shape[1] for part in flat) // 2
    bd, size = 512, tokens // 8

    def body(place_ref, w, total_ref, *rest):
        keep, give, hid = rest[-3:]
        pl.when(pl.program_id(0) == 0)(lambda: join(place_ref, rest[:len(flat)], hid))
        value = dot32(hid[...], w[...], NT) + total_ref[...]

        def put(core):
            for k in range(4):
                rows = slice(k * size, (k + 1) * size)
                mine, theirs = (2 * k + core) * size, (2 * k + 1 - core) * size
                keep[rows, :] = value[mine:mine + size]
                give[rows, :] = value[theirs:theirs + size].astype(give.dtype)

        choose(place_ref, CORE, put, 1, 0)

    assert start % width == 0
    block = pl.BlockSpec((tokens // 2, bd), lambda i, s: (0, i))
    return call(
        body, place, model // bd,
        [
            pl.BlockSpec((bd, width), lambda i, s: (i, start // width)),
            pl.BlockSpec((tokens, bd), lambda i, s: (0, i)),
        ] + [whole(*part.shape) for part in flat],
        [block, block], [shape32(tokens // 2, model), shape16(tokens // 2, model)],
        [w_in, total] + flat, after, scratch=[pltpu.VMEM((tokens, width), jnp.bfloat16)], vmem=LARGE,
    )


def row_first(place, keep, got, after):
    rows, model = keep.shape
    size, cut = rows // 4, model // 2

    def body(place_ref, keep_ref, got_ref, keep_l, give_l, keep_r, give_r):
        def put(which):
            left, mine = which
            out, give = (keep_l, give_l) if left else (keep_r, give_r)
            for n in range(2):
                own, other = (2 * n + mine, 2 * n + 1 - mine) if left else (2 * mine + n, 2 * (1 - mine) + n)
                for k, ref in ((own, out), (other, give)):
                    part = slice(k * size, (k + 1) * size)
                    value = keep_ref[part, :] + got_ref[part, :].astype(jnp.float32)
                    ref[n * size:(n + 1) * size, :] = value.astype(ref.dtype)

        pl.when(pl.program_id(0) == 0)(lambda: choose(place_ref, X, put, (True, 1), (True, 0)))
        pl.when(pl.program_id(0) == 1)(lambda: choose(place_ref, Y, put, (False, 1), (False, 0)))

    block = pl.BlockSpec((rows, cut), lambda i, s: (0, i))
    return call(
        body, place, 2, [block, block], [whole(rows // 2, cut)] * 4,
        [shape32(rows // 2, cut), shape16(rows // 2, cut)] * 2, (keep, got), after,
    )


def row_second(place, keep_l, got_l, keep_r, got_r, after):
    rows, cut = keep_l.shape
    size = rows // 2

    def body(place_ref, *refs):
        for n, which in enumerate((Y, X)):
            keep_ref, got_ref, out, give = refs[2 * n], refs[2 * n + 1], refs[4 + 2 * n], refs[5 + 2 * n]

            def put(mine):
                for k, ref in ((mine, out), (1 - mine, give)):
                    part = slice(k * size, (k + 1) * size)
                    ref[...] = (keep_ref[part, :] + got_ref[part, :].astype(jnp.float32)).astype(ref.dtype)

            choose(place_ref, which, put, 1, 0)

    return call(
        body, place, 1, [whole(rows, cut)] * 4, [whole(size, cut)] * 4,
        [shape32(size, cut), shape16(size, cut)] * 2, (keep_l, got_l, keep_r, got_r), after,
    )


def row_third(place, keep_l, got_l, keep_r, got_r, after):
    size, cut = keep_l.shape

    def body(place_ref, a, b, c, d, out):
        out[:, :cut] = (a[...] + b[...].astype(jnp.float32)).astype(out.dtype)
        out[:, cut:] = (c[...] + d[...].astype(jnp.float32)).astype(out.dtype)

    return call(
        body, place, 1, [whole(size, cut)] * 4, [whole(size, 2 * cut)], [shape16(size, 2 * cut)],
        (keep_l, got_l, keep_r, got_r), after,
    )


ROW, COL = 8, 4
PAIRS = [(COL * r + c, COL * r + (c ^ 1)) for r in range(ROW) for c in range(COL)]
OUTWARD = [(COL * r + c, COL * r + (c ^ 1)) for r in range(ROW) for c in (0, 3)]
MIDDLE = [(COL * r + c, COL * r + 3 - c) for r in range(ROW) for c in (1, 2)] + [
    (COL * r + c, COL * (r ^ 1) + c) for r in range(ROW) for c in (0, 3)
]
WIDTH, PIECE = 512, 1024
WITH = {"I0": 1, "I1": 2, "C0": 3, "C1": 4, "C2": 5}
ORDER = (
    "O0", "O1", "O2", "A0", "N0", "A1", "N1", "I0", "B0", "N2", "A2", "I1", "A3", "A4", "V0", "B1", "C0", "V1", "B2",
    "A5", "C1", "V2", "B3", "W0", "C2", "B4", "V3", "C3", "W1", "W2", "B5", "C4", "W3", "C5", "T0", "I2", "T1", "W4",
    "R1", "W5", "V4", "R2", "V5", "R3",
)


def send(value, perm):
    return lax.ppermute(value, ("row", "col"), perm)


def swap(value, bit):
    return lax.ppermute(value, "row", [(i, i ^ bit) for i in range(ROW)])


def on_a_line(inputs, out_grad, pre_act, w_in, w_out):
    hidden = w_in.shape[1]
    scale = 1.0 / math.sqrt(inputs.shape[0])
    row, col = lax.axis_index("row"), lax.axis_index("col")
    outer = (col == 0) | (col == 3)
    place = jnp.stack([col // 2, col % 2, outer, row % 2, (row // 2) % 2, row // 4]).astype(jnp.int32)
    own, other, near, cross, far = {}, {}, {}, {}, {}
    share, got1, got2, hid, got3 = {}, {}, {}, {}, {}
    grad_w_in = grad_w_out = total = None
    after = jnp.zeros((8, 128), jnp.float32)
    for step in ORDER:
        kind, j = step[0], int(step[1:])
        out_with = WITH.get(step)
        if kind == "A":
            share[j], after = act_partial(place, out_grad, w_out, j * WIDTH, WIDTH, after)
            if j not in WITH.values():
                got1[j] = send(share[j], OUTWARD)
        elif kind == "O":
            own[j], after = own_piece(place, pre_act, j * PIECE, PIECE, after)
            other[j] = send(own[j], PAIRS)
        elif kind == "N":
            near[j], after = near_half(place, own[j], other[j], after)
            cross[j] = send(near[j], MIDDLE)
        elif kind == "I":
            if out_with is None:
                cross[j], after = gate(place, cross[j], after)
                far[j] = send(cross[j], PAIRS)
            else:
                both, after = either(place, share[out_with], cross[j], after)
                far[j] = got1[out_with] = send(both, PAIRS)
        elif kind == "B":
            both, after = add_partials(place, share[j], got1[j], after)
            got2[j] = send(both, MIDDLE)
        elif kind == "C":
            p, half_of = j * WIDTH // PIECE, j * WIDTH % PIECE // WIDTH
            outers = None if out_with is None else share[out_with]
            hid[j], after = hid_part(place, share[j], got1[j], got2[j], near[p], cross[p], half_of, outers, after)
            got3[j] = send(hid[j], PAIRS)
            if out_with is not None:
                got1[out_with] = got3[j]
        elif kind == "V":
            p, half_of = j * WIDTH // PIECE, j * WIDTH % PIECE // WIDTH
            grad_w_out, after = out_weight(
                place, near[p], cross[p], far[p], half_of, out_grad, j * WIDTH, hidden, scale, grad_w_out, after
            )
        elif kind == "W":
            grad_w_in, after = in_weight(
                place, inputs, [(hid[j], got3[j])], j * WIDTH, hidden, scale, grad_w_in, after
            )
        elif step == "T0":
            total, after = in_partial(place, [(hid[k], got3[k]) for k in (0, 1, 2, 3)], w_in, 0, after)
        elif step == "T1":
            parts = [(hid[k], got3[k]) for k in (4, 5)]
            keep, give, after = in_last(place, parts, w_in, 4 * WIDTH, total, after)
            got = swap(give, 1)
        elif step == "R1":
            keep_l, give_l, keep_r, give_r, after = row_first(place, keep, got, after)
            got_l, got_r = swap(give_l, 2), swap(give_r, 4)
        elif step == "R2":
            keep_l, give_l, keep_r, give_r, after = row_second(place, keep_l, got_l, keep_r, got_r, after)
            got_l, got_r = swap(give_l, 4), swap(give_r, 2)
        elif step == "R3":
            grad_inputs, after = row_third(place, keep_l, got_l, keep_r, got_r, after)
    return grad_inputs, grad_w_in, grad_w_out


def anywhere(inputs, out_grad, pre_act, w_in, w_out):
    scale = 1.0 / math.sqrt(inputs.shape[0])
    act_share = lax.psum_scatter(dot32(out_grad, w_out, NT), "col", scatter_dimension=0, tiled=True)
    local_act, local_deriv = gelu_parts(pre_act)
    hid_share = (act_share * local_deriv).astype(jnp.bfloat16)
    activ_all = lax.all_gather(local_act.astype(jnp.bfloat16), "col", axis=0, tiled=True)
    hid_all = lax.all_gather(hid_share, "col", axis=0, tiled=True)
    rows = (((0,), (0,)), ((), ()))
    grad_w_out = (dot32(activ_all, out_grad, rows) * scale).astype(jnp.bfloat16)
    grad_w_in = (dot32(inputs, hid_all, rows) * scale).astype(jnp.bfloat16)
    grad_inputs = lax.psum_scatter(dot32(hid_all, w_in, NT), "row", scatter_dimension=0, tiled=True)
    return (grad_inputs.astype(jnp.bfloat16), grad_w_in, grad_w_out)


def solution(mesh):
    placed = (P(None, "col"), P(None, "col"), P("col", "row"), P("col", "row"), P("row", "col"))
    line = mesh.shape["col"] == 4 and mesh.shape["row"] == 8
    return jax.shard_map(
        on_a_line if line else anywhere,
        mesh=mesh,
        in_specs=placed,
        out_specs=(P("row", "col"), P("col", "row"), P("row", "col")),
        check_vma=False,
    )
```

time: 465 us -> 253 us (0.54)
  waiting for transfers between devices: 334 us -> 15 us
  Pallas kernels: 0 us -> 143 us
  matrix products: 84.2 us -> 0 us
  starting transfers between devices: 0.34 us -> 80.5 us
  local copies, waits for them, and re-layouts: 24.6 us -> 10.2 us
  between operations: 13.8 us -> 1.58 us
  other arithmetic: 6.9 us -> 0.01 us
    reduce_scatter x2 -> x0, waiting for transfers between devices: 221 us -> none  [the longest x1 164 us: per_device(): lax.psum_scatter(lax.dot_general(block, w_out, (((1,), (1,)), ((), ())),...]
    pallas_call x0 -> x44, Pallas kernels: none -> 143 us  [call(): pl.pallas_call(kernel, grid_spec=pltpu.PrefetchScalarGridSpec(num_scalar_...]
    all_gather x2 -> x0, waiting for transfers between devices: 112 us -> none  [the longest x1 89.4 us: per_device(): lax.all_gather(hid_share, 'col', axis=0, tiled=True)]
    dot_general x4 -> x0, matrix products: 84.2 us -> none  [the longest x1 21.1 us: per_device(): lax.dot_general(block, w_in, (((1,), (1,)), ((), ())), preferred_element_...]
    ppermute x0 -> x27, starting transfers between devices: none -> 80.5 us  [the longest x22 74.4 us: send(): return lax.ppermute(value, ('row', 'col'), perm)]
    ppermute x0 -> x27, waiting for transfers between devices: none -> 15 us  [the longest x22 14.4 us: send(): return lax.ppermute(value, ('row', 'col'), perm)]
    unnamed x3 -> x26, local copies, waits for them, and re-layouts: 24.6 us -> 10.2 us
    convert_element_type x2 -> x0, other arithmetic: 6.9 us -> none  [the longest x1 4.75 us: per_device(): local_act.astype(jnp.bfloat16)]
  transfers between devices with their start and end apart: 4 -> 27, of which waited for: 4 -> 6; matrix products, arithmetic and copies ran while one was open for 19% -> 0% of each run, Pallas kernels for 0% -> 51%
where the time goes in v1:
time: 253 us; the launch traced here: 250 us
  Pallas kernels  143 us (57%)
  starting transfers between devices  80.5 us (32%)
  waiting for transfers between devices  15 us (6%)
  local copies, waits for them, and re-layouts  10.2 us (4%)
    pallas_call x44, Pallas kernels, call(): pl.pallas_call(kernel, grid_spec=pltpu.PrefetchScalarGridSpec(num_scalar_...  143 us
    ppermute x22, starting transfers between devices, send(): return lax.ppermute(value, ('row', 'col'), perm)  74.4 us
    ppermute x22, waiting for transfers between devices, send(): return lax.ppermute(value, ('row', 'col'), perm)  14.4 us
    unnamed x26, local copies, waits for them, and re-layouts  10.2 us
    ppermute x5, starting transfers between devices, swap(): return lax.ppermute(value, 'row', [(i, i ^ bit) for i in range(ROW)])  6.16 us
  transfers between devices with their start and end apart: 27, of which 6 were waited for; matrix products, arithmetic and copies ran while one was open for 0% of the time, Pallas kernels for 51%

profile of v1, /device:TPU:0, one launch (start us, length us, event | category | flops | bytes accessed | tf_op | source)
XLA Modules:
  0.0 250.3 jit_solution(9636048509684461827)
XLA Ops:
  0.8 1.3 copy-done.2
  2.6 3.1 %collective-permute-start.1 = (bf16[192,1024]{1,0:T(8,128)(2,1)S(1)}, bf16[192,1024]{1,0:T(8,128)(2,1)S(1)}, u32[]{:S(2)}, u32[]{:S(2)}) collective-permute-start(bf16[192,1024]{1,0:T(8,128)(2,1)S(1)} %get-tuple-element.101.refs_0_), channel_id=1, source_target_pairs={{0,1},{1,0},{2,3},{3,2},{4,5},{5,4},{6,7},{7,6},{8,9},{9,8},{10,11... | collective-permute-start | bytes 1179656 | tf_op jit(solution)/shard_map/ppermute | solution.py:389
  7.0 2.3 copy-done
  9.3 5.1 %shard_map.79 = (bf16[768,512]{1,0:T(8,128)(2,1)S(1)}, f32[8,128]{1,0:T(8,128)S(1)}) custom-call(s32[6]{0:T(128)S(1)} %stack.31.place_ref, bf16[768,3072]{1,0:T(8,128)(2,1)S(1)} %copy-done, bf16[3072,3072]{1,0:T(8,128)(2,1)} %refs_1_.11, f32[8,128]{1,0:T(8,128)S(1)} %get-tuple-element.99.refs_2_), custom_call_target="tpu_custom_call" | custom-call | tf_op jit(solution)/shard_map/pallas_call | solution.py:45
  14.4 1.2 collective-permute-done.1.refs_1_
  16.4 5.6 %collective-permute-start = (bf16[768,512]{1,0:T(8,128)(2,1)S(1)}, bf16[768,512]{1,0:T(8,128)(2,1)S(1)}, u32[]{:S(2)}, u32[]{:S(2)}) collective-permute-start(bf16[768,512]{1,0:T(8,128)(2,1)S(1)} %get-tuple-element.100.refs_0_), channel_id=1, source_target_pairs={{0,1},{3,2},{4,5},{7,6},{8,9},{11,10},{12,13},{15,14},{16,17},{19,... | collective-permute-start | bytes 2359304 | tf_op jit(solution)/shard_map/ppermute | solution.py:389
  22.0 4.8 %shard_map.81 = (bf16[768,512]{1,0:T(8,128)(2,1)S(1)}, f32[8,128]{1,0:T(8,128)S(1)}) custom-call(s32[6]{0:T(128)S(1)} %stack.31.place_ref, bf16[768,3072]{1,0:T(8,128)(2,1)S(1)} %bitcast.7, bf16[3072,3072]{1,0:T(8,128)(2,1)} %refs_1_.11, f32[8,128]{1,0:T(8,128)S(1)} %get-tuple-element.103.refs_2_), custom_call_target="tpu_custom_call" | custom-call | tf_op jit(solution)/shard_map/pallas_call | solution.py:45
  27.5 0.9 collective-permute-start.5
  28.4 0.7 shard_map.83
  29.1 10.5 %collective-permute-start.7 = (bf16[768,512]{1,0:T(8,128)(2,1)S(1)}, bf16[768,512]{1,0:T(8,128)(2,1)S(1)}, u32[]{:S(2)}, u32[]{:S(2)}) collective-permute-start(bf16[768,512]{1,0:T(8,128)(2,1)S(1)} %get-tuple-element.119), channel_id=1, source_target_pairs={{0,1},{1,0},{2,3},{3,2},{4,5},{5,4},{6,7},{7,6},{8,9},{9,8},{10,11... | collective-permute-start | bytes 2359304 | tf_op jit(solution)/shard_map/ppermute | solution.py:389
  39.6 0.9 collective-permute-done.refs_1_
  40.5 0.8 shard_map.84
  41.4 7.6 %collective-permute-done.5.refs_1_ = bf16[192,1024]{1,0:T(8,128)(2,1)S(1)} collective-permute-done((bf16[192,1024]{1,0:T(8,128)(2,1)S(1)}, bf16[192,1024]{1,0:T(8,128)(2,1)S(1)}, u32[]{:S(2)}, u32[]{:S(2)}) %collective-permute-start.5) | collective-permute-done | bytes 393248 | tf_op jit(solution)/shard_map/ppermute | solution.py:389
  49.0 0.8 shard_map.85
  49.7 4.9 %shard_map.86 = (bf16[768,512]{1,0:T(8,128)(2,1)S(1)}, f32[8,128]{1,0:T(8,128)S(1)}) custom-call(s32[6]{0:T(128)S(1)} %stack.31.place_ref, bf16[768,3072]{1,0:T(8,128)(2,1)S(1)} %bitcast.7, bf16[3072,3072]{1,0:T(8,128)(2,1)} %refs_1_.11, f32[8,128]{1,0:T(8,128)S(1)} %get-tuple-element.113.refs_2_), custom_call_target="tpu_custom_call" | custom-call | tf_op jit(solution)/shard_map/pallas_call | solution.py:45
  54.6 0.7 shard_map.87
  55.3 2.5 %collective-permute-start.10 = (bf16[768,512]{1,0:T(8,128)(2,1)S(1)}, bf16[768,512]{1,0:T(8,128)(2,1)S(1)}, u32[]{:S(2)}, u32[]{:S(2)}) collective-permute-start(bf16[768,512]{1,0:T(8,128)(2,1)S(1)} %get-tuple-element.127), channel_id=1, source_target_pairs={{0,1},{1,0},{2,3},{3,2},{4,5},{5,4},{6,7},{7,6},{8,9},{9,8},{10,11... | collective-permute-start | bytes 2359304 | tf_op jit(solution)/shard_map/ppermute | solution.py:389
  57.8 4.8 %shard_map.88 = (bf16[768,512]{1,0:T(8,128)(2,1)S(1)}, f32[8,128]{1,0:T(8,128)S(1)}) custom-call(s32[6]{0:T(128)S(1)} %stack.31.place_ref, bf16[768,3072]{1,0:T(8,128)(2,1)S(1)} %bitcast.7, bf16[3072,3072]{1,0:T(8,128)(2,1)} %refs_1_.11, f32[8,128]{1,0:T(8,128)S(1)} %get-tuple-element.117.refs_2_), custom_call_target="tpu_custom_call" | custom-call | tf_op jit(solution)/shard_map/pallas_call | solution.py:45
  62.7 4.9 %shard_map.89 = (bf16[768,512]{1,0:T(8,128)(2,1)S(1)}, f32[8,128]{1,0:T(8,128)S(1)}) custom-call(s32[6]{0:T(128)S(1)} %stack.31.place_ref, bf16[768,3072]{1,0:T(8,128)(2,1)S(1)} %bitcast.7, bf16[3072,3072]{1,0:T(8,128)(2,1)} %refs_1_.11, f32[8,128]{1,0:T(8,128)S(1)} %get-tuple-element.120.refs_2_), custom_call_target="tpu_custom_call" | custom-call | tf_op jit(solution)/shard_map/pallas_call | solution.py:45
  67.5 6.3 %shard_map.90 = (bf16[3072,3072]{1,0:T(8,128)(2,1)}, f32[8,128]{1,0:T(8,128)S(1)}) custom-call(s32[6]{0:T(128)S(1)} %stack.31.place_ref, bf16[768,512]{1,0:T(8,128)(2,1)S(1)} %get-tuple-element.105.refs_0_.refs_3_, bf16[768,512]{1,0:T(8,128)(2,1)S(1)} %collective-permute-done.2.refs_1_.refs_4_, bf16[768,512]{1,0:T(8,128)(2,1)S(1)} %collective-permute-done.7.refs_2_.refs_1_, ...), custom_call_target="tpu_custom_call" | custom-call | tf_op jit(solution)/shard_map/pallas_call | solution.py:45
  73.8 0.8 shard_map.91
  74.7 0.7 shard_map.92
  75.4 3.6 %collective-permute-start.8 = (bf16[768,512]{1,0:T(8,128)(2,1)S(1)}, bf16[768,512]{1,0:T(8,128)(2,1)S(1)}, u32[]{:S(2)}, u32[]{:S(2)}) collective-permute-start(bf16[768,512]{1,0:T(8,128)(2,1)S(1)} %get-tuple-element.124.refs_1_), channel_id=1, source_target_pairs={{0,1},{1,0},{2,3},{3,2},{4,5},{5,4},{6,7},{7,6},{8,9},{9,8},{10,11... | collective-permute-start | bytes 2359304 | tf_op jit(solution)/shard_map/ppermute | solution.py:389
  79.0 6.3 %shard_map.93 = (bf16[3072,3072]{1,0:T(8,128)(2,1)}, f32[8,128]{1,0:T(8,128)S(1)}) custom-call(s32[6]{0:T(128)S(1)} %stack.31.place_ref, bf16[768,512]{1,0:T(8,128)(2,1)S(1)} %get-tuple-element.105.refs_0_.refs_3_, bf16[768,512]{1,0:T(8,128)(2,1)S(1)} %collective-permute-done.2.refs_1_.refs_4_, ...), custom_call_target="tpu_custom_call", output_to_operand_aliasing={{0}: (6, {})} | custom-call | tf_op jit(solution)/shard_map/pallas_call | solution.py:45
  85.3 0.8 shard_map.94
  86.2 4.9 %shard_map.95 = (bf16[768,512]{1,0:T(8,128)(2,1)S(1)}, f32[8,128]{1,0:T(8,128)S(1)}) custom-call(s32[6]{0:T(128)S(1)} %stack.31.place_ref, bf16[768,3072]{1,0:T(8,128)(2,1)S(1)} %bitcast.7, bf16[3072,3072]{1,0:T(8,128)(2,1)} %refs_1_.11, f32[8,128]{1,0:T(8,128)S(1)} %get-tuple-element.131.refs_2_), custom_call_target="tpu_custom_call" | custom-call | tf_op jit(solution)/shard_map/pallas_call | solution.py:45
  91.1 0.7 shard_map.96
  91.7 6.2 %collective-permute-start.11 = (bf16[768,512]{1,0:T(8,128)(2,1)S(1)}, bf16[768,512]{1,0:T(8,128)(2,1)S(1)}, u32[]{:S(2)}, u32[]{:S(2)}) collective-permute-start(bf16[768,512]{1,0:T(8,128)(2,1)S(1)} %get-tuple-element.133.refs_1_.refs_3_), channel_id=1, source_target_pairs={{0,1},{1,0},{2,3},{3,2},{4,5},{5,4},{6,7},{7,6},{8,9},{9,8},{10,11... | collective-permute-start | bytes 2359304 | tf_op jit(solution)/shard_map/ppermute | solution.py:389
  97.9 6.3 %shard_map.97 = (bf16[3072,3072]{1,0:T(8,128)(2,1)}, f32[8,128]{1,0:T(8,128)S(1)}) custom-call(s32[6]{0:T(128)S(1)} %stack.31.place_ref, bf16[768,512]{1,0:T(8,128)(2,1)S(1)} %get-tuple-element.115.refs_0_.refs_3_, bf16[768,512]{1,0:T(8,128)(2,1)S(1)} %collective-permute-done.6.refs_1_.refs_4_, ...), custom_call_target="tpu_custom_call", output_to_operand_aliasing={{0}: (6, {})} | custom-call | tf_op jit(solution)/shard_map/pallas_call | solution.py:45
  104.2 1.0 shard_map.98
  105.3 5.0 %shard_map.99 = (bf16[3072,3072]{1,0:T(8,128)(2,1)}, f32[8,128]{1,0:T(8,128)S(1)}) custom-call(s32[6]{0:T(128)S(1)} %stack.31.place_ref, bf16[768,3072]{1,0:T(8,128)(2,1)S(1)} %bitcast.9, bf16[768,512]{1,0:T(8,128)(2,1)S(1)} %get-tuple-element.124.refs_1_, bf16[768,512]{1,0:T(8,128)(2,1)S(1)} %collective-permute-done.8.refs_1_.refs_2_, ...), custom_call_target="tpu_custom_call" | custom-call | tf_op jit(solution)/shard_map/pallas_call | solution.py:45
  110.3 0.7 shard_map.100
  111.0 3.8 %collective-permute-start.13 = (bf16[768,512]{1,0:T(8,128)(2,1)S(1)}, bf16[768,512]{1,0:T(8,128)(2,1)S(1)}, u32[]{:S(2)}, u32[]{:S(2)}) collective-permute-start(bf16[768,512]{1,0:T(8,128)(2,1)S(1)} %get-tuple-element.141.refs_1_.refs_5_), channel_id=1, source_target_pairs={{0,1},{1,0},{2,3},{3,2},{4,5},{5,4},{6,7},{7,6},{8,9},{9,8},{10,11... | collective-permute-start | bytes 2359304 | tf_op jit(solution)/shard_map/ppermute | solution.py:389
  114.8 1.6 collective-permute-done.11.refs_1_.refs_2_.refs_4_
  116.4 0.8 shard_map.101
  117.1 6.3 %shard_map.102 = (bf16[3072,3072]{1,0:T(8,128)(2,1)}, f32[8,128]{1,0:T(8,128)S(1)}) custom-call(s32[6]{0:T(128)S(1)} %stack.31.place_ref, bf16[768,512]{1,0:T(8,128)(2,1)S(1)} %get-tuple-element.115.refs_0_.refs_3_, bf16[768,512]{1,0:T(8,128)(2,1)S(1)} %collective-permute-done.6.refs_1_.refs_4_, ...), custom_call_target="tpu_custom_call", output_to_operand_aliasing={{0}: (6, {})} | custom-call | tf_op jit(solution)/shard_map/pallas_call | solution.py:45
  123.5 0.7 shard_map.103
  124.1 7.5 %collective-permute-start.15 = (bf16[768,512]{1,0:T(8,128)(2,1)S(1)}, bf16[768,512]{1,0:T(8,128)(2,1)S(1)}, u32[]{:S(2)}, u32[]{:S(2)}) collective-permute-start(bf16[768,512]{1,0:T(8,128)(2,1)S(1)} %get-tuple-element.147.refs_1_.refs_7_), channel_id=1, source_target_pairs={{0,1},{1,0},{2,3},{3,2},{4,5},{5,4},{6,7},{7,6},{8,9},{9,8},{10,11... | collective-permute-start | bytes 2359304 | tf_op jit(solution)/shard_map/ppermute | solution.py:389
  131.6 5.0 %shard_map.104 = (bf16[3072,3072]{1,0:T(8,128)(2,1)}, f32[8,128]{1,0:T(8,128)S(1)}) custom-call(s32[6]{0:T(128)S(1)} %stack.31.place_ref, bf16[768,3072]{1,0:T(8,128)(2,1)S(1)} %bitcast.9, bf16[768,512]{1,0:T(8,128)(2,1)S(1)} %get-tuple-element.133.refs_1_.refs_3_, ...), custom_call_target="tpu_custom_call", output_to_operand_aliasing={{0}: (4, {})} | custom-call | tf_op jit(solution)/shard_map/pallas_call | solution.py:45
  136.6 5.0 %shard_map.105 = (bf16[3072,3072]{1,0:T(8,128)(2,1)}, f32[8,128]{1,0:T(8,128)S(1)}) custom-call(s32[6]{0:T(128)S(1)} %stack.31.place_ref, bf16[768,3072]{1,0:T(8,128)(2,1)S(1)} %bitcast.9, bf16[768,512]{1,0:T(8,128)(2,1)S(1)} %get-tuple-element.141.refs_1_.refs_5_, ...), custom_call_target="tpu_custom_call", output_to_operand_aliasing={{0}: (4, {})} | custom-call | tf_op jit(solution)/shard_map/pallas_call | solution.py:45
  141.6 0.8 shard_map.106
  143.0 0.7 shard_map.107
  143.6 21.7 %collective-permute-start.19 = (bf16[768,512]{1,0:T(8,128)(2,1)S(1)}, bf16[768,512]{1,0:T(8,128)(2,1)S(1)}, u32[]{:S(2)}, u32[]{:S(2)}) collective-permute-start(bf16[768,512]{1,0:T(8,128)(2,1)S(1)} %get-tuple-element.162.refs_2_.refs_1_), channel_id=1, source_target_pairs={{0,1},{1,0},{2,3},{3,2},{4,5},{5,4},{6,7},{7,6},{8,9},{9,8},{10,11... | collective-permute-start | bytes 2359304 | tf_op jit(solution)/shard_map/ppermute | solution.py:389
  165.3 5.0 %shard_map.108 = (bf16[3072,3072]{1,0:T(8,128)(2,1)}, f32[8,128]{1,0:T(8,128)S(1)}) custom-call(s32[6]{0:T(128)S(1)} %stack.31.place_ref, bf16[768,3072]{1,0:T(8,128)(2,1)S(1)} %bitcast.9, bf16[768,512]{1,0:T(8,128)(2,1)S(1)} %get-tuple-element.147.refs_1_.refs_7_, ...), custom_call_target="tpu_custom_call", output_to_operand_aliasing={{0}: (4, {})} | custom-call | tf_op jit(solution)/shard_map/pallas_call | solution.py:45
  170.3 0.9 shard_map.109
  171.2 8.0 %collective-permute-start.20 = (bf16[768,512]{1,0:T(8,128)(2,1)S(1)}, bf16[768,512]{1,0:T(8,128)(2,1)S(1)}, u32[]{:S(2)}, u32[]{:S(2)}) collective-permute-start(bf16[768,512]{1,0:T(8,128)(2,1)S(1)} %get-tuple-element.163.refs_4_.refs_1_), channel_id=1, source_target_pairs={{0,1},{1,0},{2,3},{3,2},{4,5},{5,4},{6,7},{7,6},{8,9},{9,8},{10,11... | collective-permute-start | bytes 2359304 | tf_op jit(solution)/shard_map/ppermute | solution.py:389
  179.2 15.4 %shard_map.110 = (f32[768,3072]{1,0:T(8,128)}, f32[8,128]{1,0:T(8,128)S(1)}) custom-call(s32[6]{0:T(128)S(1)} %stack.31.place_ref, bf16[3072,3072]{1,0:T(8,128)(2,1)} %refs_0_.31, bf16[768,512]{1,0:T(8,128)(2,1)S(1)} %get-tuple-element.124.refs_1_, bf16[768,512]{1,0:T(8,128)(2,1)S(1)} %collective-permute-done.8.refs_1_.refs_2_, ...), custom_call_target="tpu_custom_call" | custom-call | tf_op jit(solution)/shard_map/pallas_call | solution.py:45
  195.2 0.9 copy-done.5
  196.1 1.1 copy-done.6
  197.2 11.9 %shard_map.112 = (f32[384,3072]{1,0:T(8,128)S(1)}, bf16[384,3072]{1,0:T(8,128)(2,1)}, f32[8,128]{1,0:T(8,128)S(1)}) custom-call(s32[6]{0:T(128)S(1)} %stack.31.place_ref, bf16[3072,3072]{1,0:T(8,128)(2,1)} %refs_0_.31, f32[768,3072]{1,0:T(8,128)} %get-tuple-element.161.refs_1_, bf16[768,512]{1,0:T(8,128)(2,1)S(1)} %get-tuple-element.162.refs_2_.refs_1_, ...), custom_call_target="tpu_custom_call" | custom-call | tf_op jit(solution)/shard_map/pallas_call | solution.py:45
  209.1 2.2 copy-done.3
  211.3 2.3 copy-done.1
  213.6 5.0 %shard_map.113 = (bf16[3072,3072]{1,0:T(8,128)(2,1)}, f32[8,128]{1,0:T(8,128)S(1)}) custom-call(s32[6]{0:T(128)S(1)} %stack.31.place_ref, bf16[768,3072]{1,0:T(8,128)(2,1)S(1)} %copy-done.1, bf16[768,512]{1,0:T(8,128)(2,1)S(1)} %get-tuple-element.162.refs_2_.refs_1_, bf16[768,512]{1,0:T(8,128)(2,1)S(1)} %copy-done.6, ...), custom_call_target="tpu_custom_call", output_to_operand_aliasing={{0}: (4, {})} | custom-call | tf_op jit(solution)/shard_map/pallas_call | solution.py:45
  218.6 1.5 shard_map.114
  220.1 1.6 collective-permute-start.22
  221.7 1.5 collective-permute-start.23
  223.2 5.0 %shard_map.115 = (bf16[3072,3072]{1,0:T(8,128)(2,1)}, f32[8,128]{1,0:T(8,128)S(1)}) custom-call(s32[6]{0:T(128)S(1)} %stack.31.place_ref, bf16[768,3072]{1,0:T(8,128)(2,1)S(1)} %bitcast.11, bf16[768,512]{1,0:T(8,128)(2,1)S(1)} %get-tuple-element.163.refs_4_.refs_1_, ...), custom_call_target="tpu_custom_call", output_to_operand_aliasing={{0}: (4, {})} | custom-call | tf_op jit(solution)/shard_map/pallas_call | solution.py:45
  228.2 3.0 %collective-permute-done.24.refs_2_ = bf16[768,512]{1,0:T(8,128)(2,1)S(1)} collective-permute-done((bf16[768,512]{1,0:T(8,128)(2,1)S(1)}, bf16[768,512]{1,0:T(8,128)(2,1)S(1)}, u32[]{:S(2)}, u32[]{:S(2)}) %collective-permute-start.24) | collective-permute-done | bytes 786464 | tf_op jit(solution)/shard_map/ppermute | solution.py:389
  231.2 6.3 %shard_map.116 = (bf16[3072,3072]{1,0:T(8,128)(2,1)}, f32[8,128]{1,0:T(8,128)S(1)}) custom-call(s32[6]{0:T(128)S(1)} %stack.31.place_ref, bf16[768,512]{1,0:T(8,128)(2,1)S(1)} %get-tuple-element.154.refs_3_.refs_0_, bf16[768,512]{1,0:T(8,128)(2,1)S(1)} %get-tuple-element.175.refs_1_, ...), custom_call_target="tpu_custom_call", output_to_operand_aliasing={{0}: (6, {})} | custom-call | tf_op jit(solution)/shard_map/pallas_call | solution.py:45
  237.6 0.8 shard_map.117
  238.4 1.6 collective-permute-start.25
  240.0 1.5 collective-permute-start.26
  241.5 6.3 %shard_map.118 = (bf16[3072,3072]{1,0:T(8,128)(2,1)}, f32[8,128]{1,0:T(8,128)S(1)}) custom-call(s32[6]{0:T(128)S(1)} %stack.31.place_ref, bf16[768,512]{1,0:T(8,128)(2,1)S(1)} %get-tuple-element.154.refs_3_.refs_0_, bf16[768,512]{1,0:T(8,128)(2,1)S(1)} %get-tuple-element.175.refs_1_, ...), custom_call_target="tpu_custom_call", output_to_operand_aliasing={{0}: (6, {})} | custom-call | tf_op jit(solution)/shard_map/pallas_call | solution.py:45
  248.3 1.5 shard_map.119
  (65 shorter events, 5.3 us)
Async XLA Ops:
  0.6 21.3 %slice-start = ((s8[4718592]{0:T(1024)(128)(4,1)}), s8[524288]{0:T(1024)(128)(4,1)S(1)}, s32[]{:S(2)}) async-start(s8[4718592]{0:T(1024)(128)(4,1)} %bitcast.6), calls=%async_computation | async-start | bytes 1048576
  0.8 1.3 copy-start.2
  2.6 13.0 %collective-permute-start.1 = (bf16[192,1024]{1,0:T(8,128)(2,1)S(1)}, bf16[192,1024]{1,0:T(8,128)(2,1)S(1)}, u32[]{:S(2)}, u32[]{:S(2)}) collective-permute-start(bf16[192,1024]{1,0:T(8,128)(2,1)S(1)} %get-tuple-element.101.refs_0_), channel_id=1, source_target_pairs={{0,1},{1,0},{2,3},{3,2},{4,5},{5,4},{6,7},{7,6},{8,9},{9,8},{10,11... | collective-permute-start | bytes 1179656 | tf_op jit(solution)/shard_map/ppermute | solution.py:389
  6.3 20.5 %collective-permute-start.3 = (bf16[192,1024]{1,0:T(8,128)(2,1)S(1)}, bf16[192,1024]{1,0:T(8,128)(2,1)S(1)}, u32[]{:S(2)}, u32[]{:S(2)}) collective-permute-start(bf16[192,1024]{1,0:T(8,128)(2,1)S(1)} %get-tuple-element.106.refs_0_), channel_id=1, source_target_pairs={{0,1},{1,0},{2,3},{3,2},{4,5},{5,4},{6,7},{7,6},{8,9},{9,8},{10,11... | collective-permute-start | bytes 1179656 | tf_op jit(solution)/shard_map/ppermute | solution.py:389
  7.0 2.3 copy-start
  9.3 12.6 %slice-start.1 = ((s8[4718592]{0:T(1024)(128)(4,1)}), s8[4194304]{0:T(1024)(128)(4,1)S(1)}, s32[]{:S(2)}) async-start(s8[4718592]{0:T(1024)(128)(4,1)} %bitcast.6), calls=%async_computation.1 | async-start | bytes 8388608
  16.3 12.1 %collective-permute-start.2 = (bf16[768,512]{1,0:T(8,128)(2,1)S(1)}, bf16[768,512]{1,0:T(8,128)(2,1)S(1)}, u32[]{:S(2)}, u32[]{:S(2)}) collective-permute-start(bf16[768,512]{1,0:T(8,128)(2,1)S(1)} %get-tuple-element.105.refs_0_.refs_3_), channel_id=1, source_target_pairs={{1,2},{2,1},{5,6},{6,5},{9,10},{10,9},{13,14},{14,13},{17,18},{18,... | collective-permute-start | bytes 2359304 | tf_op jit(solution)/shard_map/ppermute | solution.py:389
  16.4 24.2 %collective-permute-start = (bf16[768,512]{1,0:T(8,128)(2,1)S(1)}, bf16[768,512]{1,0:T(8,128)(2,1)S(1)}, u32[]{:S(2)}, u32[]{:S(2)}) collective-permute-start(bf16[768,512]{1,0:T(8,128)(2,1)S(1)} %get-tuple-element.100.refs_0_), channel_id=1, source_target_pairs={{0,1},{3,2},{4,5},{7,6},{8,9},{11,10},{12,13},{15,14},{16,17},{19,... | collective-permute-start | bytes 2359304 | tf_op jit(solution)/shard_map/ppermute | solution.py:389
  27.4 27.2 %collective-permute-start.6 = (bf16[768,512]{1,0:T(8,128)(2,1)S(1)}, bf16[768,512]{1,0:T(8,128)(2,1)S(1)}, u32[]{:S(2)}, u32[]{:S(2)}) collective-permute-start(bf16[768,512]{1,0:T(8,128)(2,1)S(1)} %get-tuple-element.115.refs_0_.refs_3_), channel_id=1, source_target_pairs={{1,2},{2,1},{5,6},{6,5},{9,10},{10,9},{13,14},{14,13},{17,18},{18,... | collective-permute-start | bytes 2359304 | tf_op jit(solution)/shard_map/ppermute | solution.py:389
  27.5 21.4 %collective-permute-start.5 = (bf16[192,1024]{1,0:T(8,128)(2,1)S(1)}, bf16[192,1024]{1,0:T(8,128)(2,1)S(1)}, u32[]{:S(2)}, u32[]{:S(2)}) collective-permute-start(bf16[192,1024]{1,0:T(8,128)(2,1)S(1)} %get-tuple-element.111.refs_0_), channel_id=1, source_target_pairs={{0,1},{1,0},{2,3},{3,2},{4,5},{5,4},{6,7},{7,6},{8,9},{9,8},{10,11... | collective-permute-start | bytes 1179656 | tf_op jit(solution)/shard_map/ppermute | solution.py:389
  29.1 38.4 %collective-permute-start.7 = (bf16[768,512]{1,0:T(8,128)(2,1)S(1)}, bf16[768,512]{1,0:T(8,128)(2,1)S(1)}, u32[]{:S(2)}, u32[]{:S(2)}) collective-permute-start(bf16[768,512]{1,0:T(8,128)(2,1)S(1)} %get-tuple-element.119), channel_id=1, source_target_pairs={{0,1},{1,0},{2,3},{3,2},{4,5},{5,4},{6,7},{7,6},{8,9},{9,8},{10,11... | collective-permute-start | bytes 2359304 | tf_op jit(solution)/shard_map/ppermute | solution.py:389
  41.3 33.4 %collective-permute-start.4 = (bf16[768,512]{1,0:T(8,128)(2,1)S(1)}, bf16[768,512]{1,0:T(8,128)(2,1)S(1)}, u32[]{:S(2)}, u32[]{:S(2)}) collective-permute-start(bf16[768,512]{1,0:T(8,128)(2,1)S(1)} %get-tuple-element.110), channel_id=1, source_target_pairs={{1,2},{2,1},{5,6},{6,5},{9,10},{10,9},{13,14},{14,13},{17,18},{18,... | collective-permute-start | bytes 2359304 | tf_op jit(solution)/shard_map/ppermute | solution.py:389
  55.3 30.1 %collective-permute-start.10 = (bf16[768,512]{1,0:T(8,128)(2,1)S(1)}, bf16[768,512]{1,0:T(8,128)(2,1)S(1)}, u32[]{:S(2)}, u32[]{:S(2)}) collective-permute-start(bf16[768,512]{1,0:T(8,128)(2,1)S(1)} %get-tuple-element.127), channel_id=1, source_target_pairs={{0,1},{1,0},{2,3},{3,2},{4,5},{5,4},{6,7},{7,6},{8,9},{9,8},{10,11... | collective-permute-start | bytes 2359304 | tf_op jit(solution)/shard_map/ppermute | solution.py:389
  74.6 16.4 %collective-permute-start.9 = (bf16[768,512]{1,0:T(8,128)(2,1)S(1)}, bf16[768,512]{1,0:T(8,128)(2,1)S(1)}, u32[]{:S(2)}, u32[]{:S(2)}) collective-permute-start(bf16[768,512]{1,0:T(8,128)(2,1)S(1)} %get-tuple-element.125), channel_id=1, source_target_pairs={{1,2},{2,1},{5,6},{6,5},{9,10},{10,9},{13,14},{14,13},{17,18},{18,... | collective-permute-start | bytes 2359304 | tf_op jit(solution)/shard_map/ppermute | solution.py:389
  75.4 28.8 %collective-permute-start.8 = (bf16[768,512]{1,0:T(8,128)(2,1)S(1)}, bf16[768,512]{1,0:T(8,128)(2,1)S(1)}, u32[]{:S(2)}, u32[]{:S(2)}) collective-permute-start(bf16[768,512]{1,0:T(8,128)(2,1)S(1)} %get-tuple-element.124.refs_1_), channel_id=1, source_target_pairs={{0,1},{1,0},{2,3},{3,2},{4,5},{5,4},{6,7},{7,6},{8,9},{9,8},{10,11... | collective-permute-start | bytes 2359304 | tf_op jit(solution)/shard_map/ppermute | solution.py:389
  86.1 24.2 %collective-permute-start.12 = (bf16[768,512]{1,0:T(8,128)(2,1)S(1)}, bf16[768,512]{1,0:T(8,128)(2,1)S(1)}, u32[]{:S(2)}, u32[]{:S(2)}) collective-permute-start(bf16[768,512]{1,0:T(8,128)(2,1)S(1)} %get-tuple-element.134), channel_id=1, source_target_pairs={{1,2},{2,1},{5,6},{6,5},{9,10},{10,9},{13,14},{14,13},{17,18},{18,... | collective-permute-start | bytes 2359304 | tf_op jit(solution)/shard_map/ppermute | solution.py:389
  91.0 14.3 %slice-start.2 = ((s8[4718592]{0:T(1024)(128)(4,1)}), s8[4194304]{0:T(1024)(128)(4,1)S(1)}, s32[]{:S(2)}) async-start(s8[4718592]{0:T(1024)(128)(4,1)} %bitcast.8), calls=%async_computation.2 | async-start | bytes 8388608
  91.7 24.6 %collective-permute-start.11 = (bf16[768,512]{1,0:T(8,128)(2,1)S(1)}, bf16[768,512]{1,0:T(8,128)(2,1)S(1)}, u32[]{:S(2)}, u32[]{:S(2)}) collective-permute-start(bf16[768,512]{1,0:T(8,128)(2,1)S(1)} %get-tuple-element.133.refs_1_.refs_3_), channel_id=1, source_target_pairs={{0,1},{1,0},{2,3},{3,2},{4,5},{5,4},{6,7},{7,6},{8,9},{9,8},{10,11... | collective-permute-start | bytes 2359304 | tf_op jit(solution)/shard_map/ppermute | solution.py:389
  97.9 7.4 %slice-start.3 = ((s8[4718592]{0:T(1024)(128)(4,1)}), s8[524288]{0:T(1024)(128)(4,1)S(1)}, s32[]{:S(2)}) async-start(s8[4718592]{0:T(1024)(128)(4,1)} %bitcast.8), calls=%async_computation.3 | async-start | bytes 1048576
  105.2 18.2 %collective-permute-start.14 = (bf16[768,512]{1,0:T(8,128)(2,1)S(1)}, bf16[768,512]{1,0:T(8,128)(2,1)S(1)}, u32[]{:S(2)}, u32[]{:S(2)}) collective-permute-start(bf16[768,512]{1,0:T(8,128)(2,1)S(1)} %get-tuple-element.142), channel_id=1, source_target_pairs={{1,2},{2,1},{5,6},{6,5},{9,10},{10,9},{13,14},{14,13},{17,18},{18,... | collective-permute-start | bytes 2359304 | tf_op jit(solution)/shard_map/ppermute | solution.py:389
  111.0 25.6 %collective-permute-start.13 = (bf16[768,512]{1,0:T(8,128)(2,1)S(1)}, bf16[768,512]{1,0:T(8,128)(2,1)S(1)}, u32[]{:S(2)}, u32[]{:S(2)}) collective-permute-start(bf16[768,512]{1,0:T(8,128)(2,1)S(1)} %get-tuple-element.141.refs_1_.refs_5_), channel_id=1, source_target_pairs={{0,1},{1,0},{2,3},{3,2},{4,5},{5,4},{6,7},{7,6},{8,9},{9,8},{10,11... | collective-permute-start | bytes 2359304 | tf_op jit(solution)/shard_map/ppermute | solution.py:389
  114.8 28.2 %collective-permute-start.17 = (bf16[768,512]{1,0:T(8,128)(2,1)S(1)}, bf16[768,512]{1,0:T(8,128)(2,1)S(1)}, u32[]{:S(2)}, u32[]{:S(2)}) collective-permute-start(bf16[768,512]{1,0:T(8,128)(2,1)S(1)} %get-tuple-element.154.refs_3_.refs_0_), channel_id=1, source_target_pairs={{1,2},{2,1},{5,6},{6,5},{9,10},{10,9},{13,14},{14,13},{17,18},{18,... | collective-permute-start | bytes 2359304 | tf_op jit(solution)/shard_map/ppermute | solution.py:389
  124.1 41.2 %collective-permute-start.15 = (bf16[768,512]{1,0:T(8,128)(2,1)S(1)}, bf16[768,512]{1,0:T(8,128)(2,1)S(1)}, u32[]{:S(2)}, u32[]{:S(2)}) collective-permute-start(bf16[768,512]{1,0:T(8,128)(2,1)S(1)} %get-tuple-element.147.refs_1_.refs_7_), channel_id=1, source_target_pairs={{0,1},{1,0},{2,3},{3,2},{4,5},{5,4},{6,7},{7,6},{8,9},{9,8},{10,11... | collective-permute-start | bytes 2359304 | tf_op jit(solution)/shard_map/ppermute | solution.py:389
  131.6 11.3 %collective-permute-start.18 = (bf16[768,512]{1,0:T(8,128)(2,1)S(1)}, bf16[768,512]{1,0:T(8,128)(2,1)S(1)}, u32[]{:S(2)}, u32[]{:S(2)}) collective-permute-start(bf16[768,512]{1,0:T(8,128)(2,1)S(1)} %get-tuple-element.156), channel_id=1, source_target_pairs={{1,2},{2,1},{5,6},{6,5},{9,10},{10,9},{13,14},{14,13},{17,18},{18,... | collective-permute-start | bytes 2359304 | tf_op jit(solution)/shard_map/ppermute | solution.py:389
  142.4 27.9 %collective-permute-start.16 = (bf16[768,512]{1,0:T(8,128)(2,1)S(1)}, bf16[768,512]{1,0:T(8,128)(2,1)S(1)}, u32[]{:S(2)}, u32[]{:S(2)}) collective-permute-start(bf16[768,512]{1,0:T(8,128)(2,1)S(1)} %get-tuple-element.153), channel_id=1, source_target_pairs={{1,2},{2,1},{5,6},{6,5},{9,10},{10,9},{13,14},{14,13},{17,18},{18,... | collective-permute-start | bytes 2359304 | tf_op jit(solution)/shard_map/ppermute | solution.py:389
  143.6 51.5 %collective-permute-start.19 = (bf16[768,512]{1,0:T(8,128)(2,1)S(1)}, bf16[768,512]{1,0:T(8,128)(2,1)S(1)}, u32[]{:S(2)}, u32[]{:S(2)}) collective-permute-start(bf16[768,512]{1,0:T(8,128)(2,1)S(1)} %get-tuple-element.162.refs_2_.refs_1_), channel_id=1, source_target_pairs={{0,1},{1,0},{2,3},{3,2},{4,5},{5,4},{6,7},{7,6},{8,9},{9,8},{10,11... | collective-permute-start | bytes 2359304 | tf_op jit(solution)/shard_map/ppermute | solution.py:389
  171.2 24.8 %collective-permute-start.20 = (bf16[768,512]{1,0:T(8,128)(2,1)S(1)}, bf16[768,512]{1,0:T(8,128)(2,1)S(1)}, u32[]{:S(2)}, u32[]{:S(2)}) collective-permute-start(bf16[768,512]{1,0:T(8,128)(2,1)S(1)} %get-tuple-element.163.refs_4_.refs_1_), channel_id=1, source_target_pairs={{0,1},{1,0},{2,3},{3,2},{4,5},{5,4},{6,7},{7,6},{8,9},{9,8},{10,11... | collective-permute-start | bytes 2359304 | tf_op jit(solution)/shard_map/ppermute | solution.py:389
  195.2 0.9 copy-start.5
  196.1 1.1 copy-start.6
  197.2 26.0 %slice-start.4 = ((s8[4718592]{0:T(1024)(128)(4,1)}), s8[524288]{0:T(1024)(128)(4,1)S(1)}, s32[]{:S(2)}) async-start(s8[4718592]{0:T(1024)(128)(4,1)} %bitcast.10), calls=%async_computation.4 | async-start | bytes 1048576
  209.1 2.2 copy-start.3
  211.3 7.4 %collective-permute-start.21 = (bf16[384,3072]{1,0:T(8,128)(2,1)}, bf16[384,3072]{1,0:T(8,128)(2,1)S(1)}, u32[]{:S(2)}, u32[]{:S(2)}) collective-permute-start(bf16[384,3072]{1,0:T(8,128)(2,1)} %get-tuple-element.167), channel_id=1, source_target_pairs={{0,4},{4,0},{8,12},{12,8},{16,20},{20,16},{24,28},{28,24},{1,5},{5... | collective-permute-start | bytes 7077896 | tf_op jit(solution)/shard_map/ppermute | solution.py:393
  211.3 20.0 %collective-permute-start.24 = (bf16[768,512]{1,0:T(8,128)(2,1)S(1)}, bf16[768,512]{1,0:T(8,128)(2,1)S(1)}, u32[]{:S(2)}, u32[]{:S(2)}) collective-permute-start(bf16[768,512]{1,0:T(8,128)(2,1)S(1)} %get-tuple-element.175.refs_1_), channel_id=1, source_target_pairs={{0,1},{1,0},{2,3},{3,2},{4,5},{5,4},{6,7},{7,6},{8,9},{9,8},{10,11... | collective-permute-start | bytes 2359304 | tf_op jit(solution)/shard_map/ppermute | solution.py:389
  211.3 2.3 copy-start.1
  213.6 5.0 %copy-start.4 = (f32[384,3072]{1,0:T(8,128)S(1)}, f32[384,3072]{1,0:T(8,128)}, u32[]{:S(2)}) copy-start(f32[384,3072]{1,0:T(8,128)} %copy-done.3) | copy-start | bytes 14155780
  213.6 9.6 %slice-start.5 = ((s8[4718592]{0:T(1024)(128)(4,1)}), s8[4194304]{0:T(1024)(128)(4,1)S(1)}, s32[]{:S(2)}) async-start(s8[4718592]{0:T(1024)(128)(4,1)} %bitcast.10), calls=%async_computation.5 | async-start | bytes 8388608
  220.1 17.4 %collective-permute-start.22 = (bf16[192,1536]{1,0:T(8,128)(2,1)S(1)}, bf16[192,1536]{1,0:T(8,128)(2,1)S(1)}, u32[]{:S(2)}, u32[]{:S(2)}) collective-permute-start(bf16[192,1536]{1,0:T(8,128)(2,1)S(1)} %get-tuple-element.172), channel_id=1, source_target_pairs={{0,8},{4,12},{8,0},{12,4},{16,24},{20,28},{24,16},{28,20},{1,9},{5... | collective-permute-start | bytes 1769480 | tf_op jit(solution)/shard_map/ppermute | solution.py:393
  221.7 15.9 %collective-permute-start.23 = (bf16[192,1536]{1,0:T(8,128)(2,1)S(1)}, bf16[192,1536]{1,0:T(8,128)(2,1)S(1)}, u32[]{:S(2)}, u32[]{:S(2)}) collective-permute-start(bf16[192,1536]{1,0:T(8,128)(2,1)S(1)} %get-tuple-element.174), channel_id=1, source_target_pairs={{0,16},{4,20},{8,24},{12,28},{16,0},{20,4},{24,8},{28,12},{1,17},{... | collective-permute-start | bytes 1769480 | tf_op jit(solution)/shard_map/ppermute | solution.py:393
  238.4 9.4 %collective-permute-start.25 = (bf16[96,1536]{1,0:T(8,128)(2,1)S(1)}, bf16[96,1536]{1,0:T(8,128)(2,1)S(1)}, u32[]{:S(2)}, u32[]{:S(2)}) collective-permute-start(bf16[96,1536]{1,0:T(8,128)(2,1)S(1)} %get-tuple-element.182), channel_id=1, source_target_pairs={{0,16},{4,20},{8,24},{12,28},{16,0},{20,4},{24,8},{28,12},{1,17},{... | collective-permute-start | bytes 884744 | tf_op jit(solution)/shard_map/ppermute | solution.py:393
  240.0 8.4 %collective-permute-start.26 = (bf16[96,1536]{1,0:T(8,128)(2,1)S(1)}, bf16[96,1536]{1,0:T(8,128)(2,1)S(1)}, u32[]{:S(2)}, u32[]{:S(2)}) collective-permute-start(bf16[96,1536]{1,0:T(8,128)(2,1)S(1)} %get-tuple-element.184), channel_id=1, source_target_pairs={{0,8},{4,12},{8,0},{12,4},{16,24},{20,28},{24,16},{28,20},{1,9},{5... | collective-permute-start | bytes 884744 | tf_op jit(solution)/shard_map/ppermute | solution.py:393

commit v2 on v1

--- a/solution.py
+++ b/solution.py
@@ -75,18 +75,26 @@
     pl.when(place_ref[which] == 0)(lambda: put(zeros))
 
 
-def act_partial(place, out_grad, w_out, start, width, after):
+def act_partial(place, out_grad, w_out, start, after):
     tokens, model = out_grad.shape
     bw = 256
-
-    def body(place_ref, grad, w, out):
-        out[...] = dot32(grad[...], w[...], NT).astype(out.dtype)
-
-    return call(
-        body, place, width // bw,
+    per = WIDTH // bw
+
+    def body(place_ref, grad, w, left, right):
+        def put(out):
+            out[...] = dot32(grad[...], w[...], NT).astype(out.dtype)
+
+        pl.when(pl.program_id(0) < per)(lambda: put(left))
+        pl.when(pl.program_id(0) >= per)(lambda: put(right))
+
+    return call(
+        body, place, 2 * per,
         [whole(tokens, model), pl.BlockSpec((bw, model), lambda i, s: (start // bw + i, 0))],
-        [pl.BlockSpec((tokens, bw), lambda i, s: (0, i))],
-        [shape16(tokens, width)], (out_grad, w_out), after, vmem=LARGE,
+        [
+            pl.BlockSpec((tokens, bw), lambda i, s: (0, jnp.minimum(i, per - 1))),
+            pl.BlockSpec((tokens, bw), lambda i, s: (0, jnp.maximum(i - per, 0))),
+        ],
+        [shape16(tokens, WIDTH)] * 2, (out_grad, w_out), after, vmem=LARGE,
     )
 
 
@@ -120,6 +128,25 @@
     )
 
 
+def near_and_relay(place, own, other, after):
+    rows, width = own.shape
+    cut = width // 2
+
+    def body(place_ref, mine, theirs, out, relay):
+        def put(pair):
+            for k in range(2):
+                for n, ref in enumerate(pair):
+                    out[(2 * k + n) * rows:(2 * k + n + 1) * rows, :] = ref[:, k * cut:(k + 1) * cut]
+
+        choose(place_ref, PLACE, put, (theirs, mine), (mine, theirs))
+        relay[...] = theirs[...]
+
+    return call(
+        body, place, 1, [whole(rows, width)] * 2, [whole(4 * rows, cut), whole(rows, width)],
+        [shape16(4 * rows, cut), shape16(rows, width)], (own, other), after,
+    )
+
+
 def gate(place, value, after):
     return call(
         lambda *refs: None, place, 1, [ANY], [ANY], [jax.ShapeDtypeStruct(value.shape, value.dtype)],
@@ -182,7 +209,7 @@
     half, model = tokens // 2, out_grad.shape[1]
     bd = 1024
 
-    def body(place_ref, near_ref, cross_ref, got_ref, og_near, og_far, *rest):
+    def body(place_ref, near_ref, cross_ref, got_ref, grad, *rest):
         out, activ = rest[-2:]
 
         @pl.when(pl.program_id(0) == 0)
@@ -190,24 +217,23 @@
             def fill(ref, first):
                 for c in range(0, half, 128):
                     value = gelu_parts(ref[c:c + 128, :])[0]
-                    activ[first + c:first + c + 128, :] = value.astype(activ.dtype)
-
-            fill(near_ref, 0)
-            choose(place_ref, OUTER, lambda ref: fill(ref, half), got_ref, cross_ref)
-
-        value = dot32(activ[:half], og_near[...], TN) + dot32(activ[half:], og_far[...], TN)
-        out[...] = (value * scale).astype(out.dtype)
-
-    operands = [near, cross, got, out_grad, out_grad]
-    specs = [pl.BlockSpec((half, width), lambda i, s: (half_of, 0))] * 3 + [
-        pl.BlockSpec((half, bd), lambda i, s: (s[SIDE], i)),
-        pl.BlockSpec((half, bd), lambda i, s: (1 - s[SIDE], i)),
-    ]
+                    rows = pl.ds(pl.multiple_of(first + c, 128), 128)
+                    activ[rows, :] = value.astype(activ.dtype)
+
+            here = place_ref[SIDE] * half
+            fill(near_ref, here)
+            choose(place_ref, OUTER, lambda ref: fill(ref, half - here), got_ref, cross_ref)
+
+        out[...] = (dot32(activ[...], grad[...], TN) * scale).astype(out.dtype)
+
+    operands = [near, cross, got, out_grad]
+    specs = [pl.BlockSpec((half, width), lambda i, s: (half_of, 0))] * 3
+    specs.append(pl.BlockSpec((tokens, bd), lambda i, s: (0, i)))
     aliases = None
     if into is not None:
         operands.append(into)
         specs.append(ANY)
-        aliases = {6: 0}
+        aliases = {5: 0}
     assert start % width == 0
     return call(
         body, place, model // bd, specs,
@@ -273,7 +299,7 @@
         [pl.BlockSpec((bd, width), lambda i, s: (i, start // width))] + [whole(*part.shape) for part in flat],
         [pl.BlockSpec((tokens, bd), lambda i, s: (0, i))],
         [shape32(tokens, model)], [w_in] + flat, after,
-        scratch=[pltpu.VMEM((tokens, width), jnp.bfloat16)], vmem=LARGE,
+        scratch=[pltpu.VMEM((tokens, width), jnp.bfloat16)],
     )
 
 
@@ -379,9 +405,9 @@
 WIDTH, PIECE = 512, 1024
 WITH = {"I0": 1, "I1": 2, "C0": 3, "C1": 4, "C2": 5}
 ORDER = (
-    "O0", "O1", "O2", "A0", "N0", "A1", "N1", "I0", "B0", "N2", "A2", "I1", "A3", "A4", "V0", "B1", "C0", "V1", "B2",
-    "A5", "C1", "V2", "B3", "W0", "C2", "B4", "V3", "C3", "W1", "W2", "B5", "C4", "W3", "C5", "T0", "I2", "T1", "W4",
-    "R1", "W5", "V4", "R2", "V5", "R3",
+    "O0", "O1", "A0", "N0", "A2", "Q0", "N1", "I0", "B0", "I1", "B1", "O2", "C0", "B2", "A4", "V0", "C1", "B3", "V1",
+    "N2", "W0", "C2", "B4", "W1", "V2", "C3", "B5", "C4", "W2", "V3", "W3", "C5", "T0", "I2", "T1", "R1", "W4", "W5",
+    "V4", "R2", "V5", "R3",
 )
 
 
@@ -407,12 +433,20 @@
         kind, j = step[0], int(step[1:])
         out_with = WITH.get(step)
         if kind == "A":
-            share[j], after = act_partial(place, out_grad, w_out, j * WIDTH, WIDTH, after)
-            if j not in WITH.values():
-                got1[j] = send(share[j], OUTWARD)
+            share[j], share[j + 1], after = act_partial(place, out_grad, w_out, j * WIDTH, after)
+            for k in (j, j + 1):
+                if k not in WITH.values():
+                    got1[k] = send(share[k], OUTWARD)
         elif kind == "O":
             own[j], after = own_piece(place, pre_act, j * PIECE, PIECE, after)
             other[j] = send(own[j], PAIRS)
+            if j == 0:
+                straight = send(own[j], MIDDLE)
+        elif step == "N0":
+            near[j], relay, after = near_and_relay(place, own[j], other[j], after)
+            relay = send(relay, MIDDLE)
+        elif step == "Q0":
+            cross[j], after = near_half(place, relay, straight, after)
         elif kind == "N":
             near[j], after = near_half(place, own[j], other[j], after)
             cross[j] = send(near[j], MIDDLE)

time: 253 us -> 247 us (0.976)
  waiting for transfers between devices: 15 us -> 43.1 us
  starting transfers between devices: 80.5 us -> 57.2 us
  Pallas kernels: 143 us -> 131 us
    ppermute x22 -> x23, waiting for transfers between devices: 14.4 us -> 37.3 us  [send(): return lax.ppermute(value, ('row', 'col'), perm)]
    ppermute x22 -> x23, starting transfers between devices: 74.4 us -> 52.8 us  [send(): return lax.ppermute(value, ('row', 'col'), perm)]
    pallas_call x44 -> x42, Pallas kernels: 143 us -> 131 us  [call(): pl.pallas_call(kernel, grid_spec=pltpu.PrefetchScalarGridSpec(num_scalar_...]
    ppermute x5, waiting for transfers between devices: 0.58 us -> 5.9 us  [swap(): return lax.ppermute(value, 'row', [(i, i ^ bit) for i in range(ROW)])]
    unnamed x26 -> x20, local copies, waits for them, and re-layouts: 10.2 us -> 11 us
  transfers between devices with their start and end apart: 27 -> 28, of which waited for: 6 -> 7; matrix products, arithmetic and copies ran while one was open for 0% -> 0% of each run, Pallas kernels for 51% -> 48%
where the time goes in v2:
time: 247 us; the launch traced here: 244 us
  Pallas kernels  131 us (53%)
  starting transfers between devices  57.2 us (23%)
  waiting for transfers between devices  43.1 us (17%)
  local copies, waits for them, and re-layouts  11.1 us (4%)
    pallas_call x42, Pallas kernels, call(): pl.pallas_call(kernel, grid_spec=pltpu.PrefetchScalarGridSpec(num_scalar_...  131 us
    ppermute x23, starting transfers between devices, send(): return lax.ppermute(value, ('row', 'col'), perm)  52.8 us
    ppermute x23, waiting for transfers between devices, send(): return lax.ppermute(value, ('row', 'col'), perm)  37.3 us
    unnamed x20, local copies, waits for them, and re-layouts  11 us
    ppermute x5, waiting for transfers between devices, swap(): return lax.ppermute(value, 'row', [(i, i ^ bit) for i in range(ROW)])  5.9 us
  transfers between devices with their start and end apart: 28, of which 7 were waited for; matrix products, arithmetic and copies ran while one was open for 0% of the time, Pallas kernels for 48%

profile of v2, /device:TPU:0, one launch (start us, length us, event | category | flops | bytes accessed | tf_op | source)
XLA Modules:
  0.0 243.7 jit_solution(8065890587919476624)
XLA Ops:
  0.8 1.3 copy-done.2
  2.6 3.1 %collective-permute-start.1 = (bf16[192,1024]{1,0:T(8,128)(2,1)S(1)}, bf16[192,1024]{1,0:T(8,128)(2,1)S(1)}, u32[]{:S(2)}, u32[]{:S(2)}) collective-permute-start(bf16[192,1024]{1,0:T(8,128)(2,1)S(1)} %get-tuple-element.101.refs_0_), channel_id=1, source_target_pairs={{0,1},{1,0},{2,3},{3,2},{4,5},{5,4},{6,7},{7,6},{8,9},{9,8},{10,11... | collective-permute-start | bytes 1179656 | tf_op jit(solution)/shard_map/ppermute | solution.py:415
  6.3 2.3 copy-done
  8.6 8.2 %shard_map.78 = (bf16[768,512]{1,0:T(8,128)(2,1)S(1)}, bf16[768,512]{1,0:T(8,128)(2,1)S(1)}, f32[8,128]{1,0:T(8,128)S(1)}) custom-call(s32[6]{0:T(128)S(1)} %stack.31.place_ref, bf16[768,3072]{1,0:T(8,128)(2,1)S(1)} %copy-done, bf16[3072,3072]{1,0:T(8,128)(2,1)} %refs_1_.5, f32[8,128]{1,0:T(8,128)S(1)} %get-tuple-element.98.refs_2_), custom_call_target="tpu_custom_call" | custom-call | tf_op jit(solution)/shard_map/pallas_call | solution.py:45
  16.8 0.6 shard_map.79
  18.1 2.7 %collective-permute-start.4 = (bf16[192,1024]{1,0:T(8,128)(2,1)S(1)}, bf16[192,1024]{1,0:T(8,128)(2,1)S(1)}, u32[]{:S(2)}, u32[]{:S(2)}) collective-permute-start(bf16[192,1024]{1,0:T(8,128)(2,1)S(1)} %get-tuple-element.107.refs_0_), channel_id=1, source_target_pairs={{0,1},{1,0},{2,3},{3,2},{4,5},{5,4},{6,7},{7,6},{8,9},{9,8},{10,11... | collective-permute-start | bytes 1179656 | tf_op jit(solution)/shard_map/ppermute | solution.py:415
  20.8 2.0 collective-permute-start
  22.8 7.9 %shard_map.80 = (bf16[768,512]{1,0:T(8,128)(2,1)S(1)}, bf16[768,512]{1,0:T(8,128)(2,1)S(1)}, f32[8,128]{1,0:T(8,128)S(1)}) custom-call(s32[6]{0:T(128)S(1)} %stack.31.place_ref, bf16[768,3072]{1,0:T(8,128)(2,1)S(1)} %bitcast.7, bf16[3072,3072]{1,0:T(8,128)(2,1)} %refs_1_.5, f32[8,128]{1,0:T(8,128)S(1)} %get-tuple-element.104.refs_2_), custom_call_target="tpu_custom_call" | custom-call | tf_op jit(solution)/shard_map/pallas_call | solution.py:45
  31.3 0.8 shard_map.82
  32.2 0.7 shard_map.83
  32.8 3.5 %collective-permute-start.6 = (bf16[768,512]{1,0:T(8,128)(2,1)S(1)}, bf16[768,512]{1,0:T(8,128)(2,1)S(1)}, u32[]{:S(2)}, u32[]{:S(2)}) collective-permute-start(bf16[768,512]{1,0:T(8,128)(2,1)S(1)} %get-tuple-element.114), channel_id=1, source_target_pairs={{0,1},{1,0},{2,3},{3,2},{4,5},{5,4},{6,7},{7,6},{8,9},{9,8},{10,11... | collective-permute-start | bytes 2359304 | tf_op jit(solution)/shard_map/ppermute | solution.py:415
  36.3 10.9 %collective-permute-done.refs_1_ = bf16[768,512]{1,0:T(8,128)(2,1)S(1)} collective-permute-done((bf16[768,512]{1,0:T(8,128)(2,1)S(1)}, bf16[768,512]{1,0:T(8,128)(2,1)S(1)}, u32[]{:S(2)}, u32[]{:S(2)}) %collective-permute-start) | collective-permute-done | bytes 786464 | tf_op jit(solution)/shard_map/ppermute | solution.py:415
  47.2 0.8 shard_map.84
  48.1 0.7 shard_map.85
  48.7 4.5 %collective-permute-start.10 = (bf16[768,512]{1,0:T(8,128)(2,1)S(1)}, bf16[768,512]{1,0:T(8,128)(2,1)S(1)}, u32[]{:S(2)}, u32[]{:S(2)}) collective-permute-start(bf16[768,512]{1,0:T(8,128)(2,1)S(1)} %get-tuple-element.123), channel_id=1, source_target_pairs={{0,1},{1,0},{2,3},{3,2},{4,5},{5,4},{6,7},{7,6},{8,9},{9,8},{10,11... | collective-permute-start | bytes 2359304 | tf_op jit(solution)/shard_map/ppermute | solution.py:415
  53.2 10.9 %collective-permute-done.6.refs_1_.refs_2_ = bf16[768,512]{1,0:T(8,128)(2,1)S(1)} collective-permute-done((bf16[768,512]{1,0:T(8,128)(2,1)S(1)}, bf16[768,512]{1,0:T(8,128)(2,1)S(1)}, u32[]{:S(2)}, u32[]{:S(2)}) %collective-permute-start.6) | collective-permute-done | bytes 786464 | tf_op jit(solution)/shard_map/ppermute | solution.py:415
  64.1 0.8 shard_map.86
  65.5 0.7 shard_map.88
  66.2 5.7 %collective-permute-start.8 = (bf16[768,512]{1,0:T(8,128)(2,1)S(1)}, bf16[768,512]{1,0:T(8,128)(2,1)S(1)}, u32[]{:S(2)}, u32[]{:S(2)}) collective-permute-start(bf16[768,512]{1,0:T(8,128)(2,1)S(1)} %get-tuple-element.121.refs_1_), channel_id=1, source_target_pairs={{0,1},{1,0},{2,3},{3,2},{4,5},{5,4},{6,7},{7,6},{8,9},{9,8},{10,11... | collective-permute-start | bytes 2359304 | tf_op jit(solution)/shard_map/ppermute | solution.py:415
  71.9 9.0 %collective-permute-done.10.refs_1_.refs_2_ = bf16[768,512]{1,0:T(8,128)(2,1)S(1)} collective-permute-done((bf16[768,512]{1,0:T(8,128)(2,1)S(1)}, bf16[768,512]{1,0:T(8,128)(2,1)S(1)}, u32[]{:S(2)}, u32[]{:S(2)}) %collective-permute-start.10) | collective-permute-done | bytes 786464 | tf_op jit(solution)/shard_map/ppermute | solution.py:415
  80.9 0.8 shard_map.89
  81.8 4.4 %collective-permute-start.13 = (bf16[192,1024]{1,0:T(8,128)(2,1)S(1)}, bf16[192,1024]{1,0:T(8,128)(2,1)S(1)}, u32[]{:S(2)}, u32[]{:S(2)}) collective-permute-start(bf16[192,1024]{1,0:T(8,128)(2,1)S(1)} %get-tuple-element.132.refs_0_), channel_id=1, source_target_pairs={{0,1},{1,0},{2,3},{3,2},{4,5},{5,4},{6,7},{7,6},{8,9},{9,8},{10,11... | collective-permute-start | bytes 1179656 | tf_op jit(solution)/shard_map/ppermute | solution.py:415
  86.2 7.9 %shard_map.90 = (bf16[768,512]{1,0:T(8,128)(2,1)S(1)}, bf16[768,512]{1,0:T(8,128)(2,1)S(1)}, f32[8,128]{1,0:T(8,128)S(1)}) custom-call(s32[6]{0:T(128)S(1)} %stack.31.place_ref, bf16[768,3072]{1,0:T(8,128)(2,1)S(1)} %bitcast.7, bf16[3072,3072]{1,0:T(8,128)(2,1)} %refs_1_.5, f32[8,128]{1,0:T(8,128)S(1)} %get-tuple-element.125.refs_2_), custom_call_target="tpu_custom_call" | custom-call | tf_op jit(solution)/shard_map/pallas_call | solution.py:45
  94.1 5.5 %shard_map.91 = (bf16[3072,3072]{1,0:T(8,128)(2,1)}, f32[8,128]{1,0:T(8,128)S(1)}) custom-call(s32[6]{0:T(128)S(1)} %stack.31.place_ref, bf16[768,512]{1,0:T(8,128)(2,1)S(1)} %get-tuple-element.112.refs_3_.refs_0_, bf16[768,512]{1,0:T(8,128)(2,1)S(1)} %get-tuple-element.106.refs_1_.refs_4_, bf16[768,512]{1,0:T(8,128)(2,1)S(1)} %collective-permute-done.6.refs_1_.refs_2_, ...), custom_call_target="tpu_custom_call" | custom-call | tf_op jit(solution)/shard_map/pallas_call | solution.py:45
  99.5 0.7 shard_map.92
  100.2 1.3 collective-permute-start.11
  101.5 0.8 shard_map.93
  102.4 5.5 %shard_map.94 = (bf16[3072,3072]{1,0:T(8,128)(2,1)}, f32[8,128]{1,0:T(8,128)S(1)}) custom-call(s32[6]{0:T(128)S(1)} %stack.31.place_ref, bf16[768,512]{1,0:T(8,128)(2,1)S(1)} %get-tuple-element.112.refs_3_.refs_0_, bf16[768,512]{1,0:T(8,128)(2,1)S(1)} %get-tuple-element.106.refs_1_.refs_4_, ...), custom_call_target="tpu_custom_call", output_to_operand_aliasing={{0}: (5, {})} | custom-call | tf_op jit(solution)/shard_map/pallas_call | solution.py:45
  107.9 0.8 shard_map.95
  108.7 5.0 %shard_map.96 = (bf16[3072,3072]{1,0:T(8,128)(2,1)}, f32[8,128]{1,0:T(8,128)S(1)}) custom-call(s32[6]{0:T(128)S(1)} %stack.31.place_ref, bf16[768,3072]{1,0:T(8,128)(2,1)S(1)} %bitcast.9, bf16[768,512]{1,0:T(8,128)(2,1)S(1)} %get-tuple-element.121.refs_1_, bf16[768,512]{1,0:T(8,128)(2,1)S(1)} %collective-permute-done.8.refs_1_.refs_2_, ...), custom_call_target="tpu_custom_call" | custom-call | tf_op jit(solution)/shard_map/pallas_call | solution.py:45
  113.7 0.7 shard_map.97
  114.4 2.1 collective-permute-start.14
  116.5 6.5 %collective-permute-done.11.refs_1_.refs_2_.refs_4_ = bf16[768,512]{1,0:T(8,128)(2,1)S(1)} collective-permute-done((bf16[768,512]{1,0:T(8,128)(2,1)S(1)}, bf16[768,512]{1,0:T(8,128)(2,1)S(1)}, u32[]{:S(2)}, u32[]{:S(2)}) %collective-permute-start.11) | collective-permute-done | bytes 786464 | tf_op jit(solution)/shard_map/ppermute | solution.py:415
  123.0 0.8 shard_map.98
  123.9 5.0 %shard_map.99 = (bf16[3072,3072]{1,0:T(8,128)(2,1)}, f32[8,128]{1,0:T(8,128)S(1)}) custom-call(s32[6]{0:T(128)S(1)} %stack.31.place_ref, bf16[768,3072]{1,0:T(8,128)(2,1)S(1)} %bitcast.9, bf16[768,512]{1,0:T(8,128)(2,1)S(1)} %get-tuple-element.129.refs_1_.refs_3_, ...), custom_call_target="tpu_custom_call", output_to_operand_aliasing={{0}: (4, {})} | custom-call | tf_op jit(solution)/shard_map/pallas_call | solution.py:45
  128.9 5.5 %shard_map.100 = (bf16[3072,3072]{1,0:T(8,128)(2,1)}, f32[8,128]{1,0:T(8,128)S(1)}) custom-call(s32[6]{0:T(128)S(1)} %stack.31.place_ref, bf16[768,512]{1,0:T(8,128)(2,1)S(1)} %get-tuple-element.116.refs_3_.refs_0_, bf16[768,512]{1,0:T(8,128)(2,1)S(1)} %collective-permute-done.7.refs_1_.refs_4_, ...), custom_call_target="tpu_custom_call", output_to_operand_aliasing={{0}: (5, {})} | custom-call | tf_op jit(solution)/shard_map/pallas_call | solution.py:45
  134.4 0.7 shard_map.101
  135.0 5.7 %collective-permute-start.16 = (bf16[768,512]{1,0:T(8,128)(2,1)S(1)}, bf16[768,512]{1,0:T(8,128)(2,1)S(1)}, u32[]{:S(2)}, u32[]{:S(2)}) collective-permute-start(bf16[768,512]{1,0:T(8,128)(2,1)S(1)} %get-tuple-element.147.refs_1_.refs_7_), channel_id=1, source_target_pairs={{0,1},{1,0},{2,3},{3,2},{4,5},{5,4},{6,7},{7,6},{8,9},{9,8},{10,11... | collective-permute-start | bytes 2359304 | tf_op jit(solution)/shard_map/ppermute | solution.py:415
  140.8 0.8 shard_map.102
  141.7 0.7 shard_map.103
  142.3 14.6 %collective-permute-start.20 = (bf16[768,512]{1,0:T(8,128)(2,1)S(1)}, bf16[768,512]{1,0:T(8,128)(2,1)S(1)}, u32[]{:S(2)}, u32[]{:S(2)}) collective-permute-start(bf16[768,512]{1,0:T(8,128)(2,1)S(1)} %get-tuple-element.162.refs_2_.refs_1_), channel_id=1, source_target_pairs={{0,1},{1,0},{2,3},{3,2},{4,5},{5,4},{6,7},{7,6},{8,9},{9,8},{10,11... | collective-permute-start | bytes 2359304 | tf_op jit(solution)/shard_map/ppermute | solution.py:415
  156.9 5.0 %shard_map.104 = (bf16[3072,3072]{1,0:T(8,128)(2,1)}, f32[8,128]{1,0:T(8,128)S(1)}) custom-call(s32[6]{0:T(128)S(1)} %stack.31.place_ref, bf16[768,3072]{1,0:T(8,128)(2,1)S(1)} %bitcast.9, bf16[768,512]{1,0:T(8,128)(2,1)S(1)} %get-tuple-element.139.refs_1_.refs_5_, ...), custom_call_target="tpu_custom_call", output_to_operand_aliasing={{0}: (4, {})} | custom-call | tf_op jit(solution)/shard_map/pallas_call | solution.py:45
  161.9 5.5 %shard_map.105 = (bf16[3072,3072]{1,0:T(8,128)(2,1)}, f32[8,128]{1,0:T(8,128)S(1)}) custom-call(s32[6]{0:T(128)S(1)} %stack.31.place_ref, bf16[768,512]{1,0:T(8,128)(2,1)S(1)} %get-tuple-element.116.refs_3_.refs_0_, bf16[768,512]{1,0:T(8,128)(2,1)S(1)} %collective-permute-done.7.refs_1_.refs_4_, ...), custom_call_target="tpu_custom_call", output_to_operand_aliasing={{0}: (5, {})} | custom-call | tf_op jit(solution)/shard_map/pallas_call | solution.py:45
  167.4 5.2 %shard_map.106 = (bf16[3072,3072]{1,0:T(8,128)(2,1)}, f32[8,128]{1,0:T(8,128)S(1)}) custom-call(s32[6]{0:T(128)S(1)} %stack.31.place_ref, bf16[768,3072]{1,0:T(8,128)(2,1)S(1)} %bitcast.9, bf16[768,512]{1,0:T(8,128)(2,1)S(1)} %get-tuple-element.147.refs_1_.refs_7_, ...), custom_call_target="tpu_custom_call", output_to_operand_aliasing={{0}: (4, {})} | custom-call | tf_op jit(solution)/shard_map/pallas_call | solution.py:45
  172.6 0.7 shard_map.107
  173.3 1.3 collective-permute-start.21
  174.6 14.0 %shard_map.108 = (f32[768,3072]{1,0:T(8,128)S(1)}, f32[8,128]{1,0:T(8,128)S(1)}) custom-call(s32[6]{0:T(128)S(1)} %stack.31.place_ref, bf16[3072,3072]{1,0:T(8,128)(2,1)} %refs_0_.25, bf16[768,512]{1,0:T(8,128)(2,1)S(1)} %get-tuple-element.121.refs_1_, bf16[768,512]{1,0:T(8,128)(2,1)S(1)} %collective-permute-done.8.refs_1_.refs_2_, ...), custom_call_target="tpu_custom_call" | custom-call | tf_op jit(solution)/shard_map/pallas_call | solution.py:45
  188.6 3.7 %copy-done.4 = f32[768,3072]{1,0:T(8,128)} copy-done((f32[768,3072]{1,0:T(8,128)}, f32[768,3072]{1,0:T(8,128)S(1)}, u32[]{:S(2)}) %copy-start.4) | copy-done | bytes 9437208
  192.9 10.9 %shard_map.110 = (f32[384,3072]{1,0:T(8,128)S(1)}, bf16[384,3072]{1,0:T(8,128)(2,1)S(1)}, f32[8,128]{1,0:T(8,128)S(1)}) custom-call(s32[6]{0:T(128)S(1)} %stack.31.place_ref, bf16[3072,3072]{1,0:T(8,128)(2,1)} %refs_0_.25, f32[768,3072]{1,0:T(8,128)} %copy-done.4, bf16[768,512]{1,0:T(8,128)(2,1)S(1)} %get-tuple-element.162.refs_2_.refs_1_, ...), custom_call_target="tpu_custom_call" | custom-call | tf_op jit(solution)/shard_map/pallas_call | solution.py:45
  203.8 1.4 copy-done.5
  205.2 0.8 collective-permute-start.25
  205.9 4.0 %collective-permute-done.22.refs_1_ = bf16[384,3072]{1,0:T(8,128)(2,1)S(1)} collective-permute-done((bf16[384,3072]{1,0:T(8,128)(2,1)}, bf16[384,3072]{1,0:T(8,128)(2,1)S(1)}, u32[]{:S(2)}, u32[]{:S(2)}) %collective-permute-start.22) | collective-permute-done | bytes 2359328 | tf_op jit(solution)/shard_map/ppermute | solution.py:419
  209.9 1.5 shard_map.111
  211.4 1.5 collective-permute-start.23
  212.9 1.5 collective-permute-start.24
  214.4 2.3 copy-done.1
  216.8 5.0 %shard_map.112 = (bf16[3072,3072]{1,0:T(8,128)(2,1)}, f32[8,128]{1,0:T(8,128)S(1)}) custom-call(s32[6]{0:T(128)S(1)} %stack.31.place_ref, bf16[768,3072]{1,0:T(8,128)(2,1)S(1)} %copy-done.1, bf16[768,512]{1,0:T(8,128)(2,1)S(1)} %get-tuple-element.162.refs_2_.refs_1_, ...), custom_call_target="tpu_custom_call", output_to_operand_aliasing={{0}: (4, {})} | custom-call | tf_op jit(solution)/shard_map/pallas_call | solution.py:45
  221.7 5.0 %shard_map.113 = (bf16[3072,3072]{1,0:T(8,128)(2,1)}, f32[8,128]{1,0:T(8,128)S(1)}) custom-call(s32[6]{0:T(128)S(1)} %stack.31.place_ref, bf16[768,3072]{1,0:T(8,128)(2,1)S(1)} %copy-done.1, bf16[768,512]{1,0:T(8,128)(2,1)S(1)} %get-tuple-element.163.refs_4_.refs_1_, ...), custom_call_target="tpu_custom_call", output_to_operand_aliasing={{0}: (4, {})} | custom-call | tf_op jit(solution)/shard_map/pallas_call | solution.py:45
  226.7 5.5 %shard_map.114 = (bf16[3072,3072]{1,0:T(8,128)(2,1)}, f32[8,128]{1,0:T(8,128)S(1)}) custom-call(s32[6]{0:T(128)S(1)} %stack.31.place_ref, bf16[768,512]{1,0:T(8,128)(2,1)S(1)} %get-tuple-element.150.refs_3_.refs_0_, bf16[768,512]{1,0:T(8,128)(2,1)S(1)} %get-tuple-element.173.refs_1_, ...), custom_call_target="tpu_custom_call", output_to_operand_aliasing={{0}: (5, {})} | custom-call | tf_op jit(solution)/shard_map/pallas_call | solution.py:45
  232.2 0.8 shard_map.115
  233.6 0.8 collective-permute-start.27
  234.4 5.5 %shard_map.116 = (bf16[3072,3072]{1,0:T(8,128)(2,1)}, f32[8,128]{1,0:T(8,128)S(1)}) custom-call(s32[6]{0:T(128)S(1)} %stack.31.place_ref, bf16[768,512]{1,0:T(8,128)(2,1)S(1)} %get-tuple-element.150.refs_3_.refs_0_, bf16[768,512]{1,0:T(8,128)(2,1)S(1)} %get-tuple-element.173.refs_1_, ...), custom_call_target="tpu_custom_call", output_to_operand_aliasing={{0}: (5, {})} | custom-call | tf_op jit(solution)/shard_map/pallas_call | solution.py:45
  239.9 1.7 collective-permute-done.26.refs_1_
  241.8 1.5 shard_map.117
  (58 shorter events, 4.9 us)
Async XLA Ops:
  0.6 22.1 %slice-start = ((s8[4718592]{0:T(1024)(128)(4,1)}), s8[524288]{0:T(1024)(128)(4,1)S(1)}, s32[]{:S(2)}) async-start(s8[4718592]{0:T(1024)(128)(4,1)} %bitcast.6), calls=%async_computation | async-start | bytes 1048576
  0.8 1.3 copy-start.2
  2.6 14.2 %collective-permute-start.1 = (bf16[192,1024]{1,0:T(8,128)(2,1)S(1)}, bf16[192,1024]{1,0:T(8,128)(2,1)S(1)}, u32[]{:S(2)}, u32[]{:S(2)}) collective-permute-start(bf16[192,1024]{1,0:T(8,128)(2,1)S(1)} %get-tuple-element.101.refs_0_), channel_id=1, source_target_pairs={{0,1},{1,0},{2,3},{3,2},{4,5},{5,4},{6,7},{7,6},{8,9},{9,8},{10,11... | collective-permute-start | bytes 1179656 | tf_op jit(solution)/shard_map/ppermute | solution.py:415
  5.7 24.9 %collective-permute-start.3 = (bf16[192,1024]{1,0:T(8,128)(2,1)S(1)}, bf16[192,1024]{1,0:T(8,128)(2,1)S(1)}, u32[]{:S(2)}, u32[]{:S(2)}) collective-permute-start(bf16[192,1024]{1,0:T(8,128)(2,1)S(1)} %get-tuple-element.101.refs_0_), channel_id=1, source_target_pairs={{1,2},{2,1},{5,6},{6,5},{9,10},{10,9},{13,14},{14,13},{17,18},{18,... | collective-permute-start | bytes 1179656 | tf_op jit(solution)/shard_map/ppermute | solution.py:415
  6.3 2.3 copy-start
  8.6 14.1 %slice-start.1 = ((s8[4718592]{0:T(1024)(128)(4,1)}), s8[4194304]{0:T(1024)(128)(4,1)S(1)}, s32[]{:S(2)}) async-start(s8[4718592]{0:T(1024)(128)(4,1)} %bitcast.6), calls=%async_computation.1 | async-start | bytes 8388608
  16.8 48.0 %copy-start.3 = (bf16[192,3072]{1,0:T(8,128)(2,1)S(1)}, bf16[192,3072]{1,0:T(8,128)(2,1)}, u32[]{:S(2)}) copy-start(bf16[192,3072]{1,0:T(8,128)(2,1)} %refs_0_.18) | copy-start | bytes 3538948
  17.5 13.2 %collective-permute-start.2 = (bf16[192,1024]{1,0:T(8,128)(2,1)S(1)}, bf16[192,1024]{1,0:T(8,128)(2,1)S(1)}, u32[]{:S(2)}, u32[]{:S(2)}) collective-permute-start(bf16[192,1024]{1,0:T(8,128)(2,1)S(1)} %get-tuple-element.103), channel_id=1, source_target_pairs={{1,2},{2,1},{5,6},{6,5},{9,10},{10,9},{13,14},{14,13},{17,18},{18,... | collective-permute-start | bytes 1179656 | tf_op jit(solution)/shard_map/ppermute | solution.py:415
  18.1 13.3 %collective-permute-start.4 = (bf16[192,1024]{1,0:T(8,128)(2,1)S(1)}, bf16[192,1024]{1,0:T(8,128)(2,1)S(1)}, u32[]{:S(2)}, u32[]{:S(2)}) collective-permute-start(bf16[192,1024]{1,0:T(8,128)(2,1)S(1)} %get-tuple-element.107.refs_0_), channel_id=1, source_target_pairs={{0,1},{1,0},{2,3},{3,2},{4,5},{5,4},{6,7},{7,6},{8,9},{9,8},{10,11... | collective-permute-start | bytes 1179656 | tf_op jit(solution)/shard_map/ppermute | solution.py:415
  20.8 26.4 %collective-permute-start = (bf16[768,512]{1,0:T(8,128)(2,1)S(1)}, bf16[768,512]{1,0:T(8,128)(2,1)S(1)}, u32[]{:S(2)}, u32[]{:S(2)}) collective-permute-start(bf16[768,512]{1,0:T(8,128)(2,1)S(1)} %get-tuple-element.99.refs_0_), channel_id=1, source_target_pairs={{0,1},{3,2},{4,5},{7,6},{8,9},{11,10},{12,13},{15,14},{16,17},{19,... | collective-permute-start | bytes 2359304 | tf_op jit(solution)/shard_map/ppermute | solution.py:415
  32.1 16.0 %collective-permute-start.7 = (bf16[768,512]{1,0:T(8,128)(2,1)S(1)}, bf16[768,512]{1,0:T(8,128)(2,1)S(1)}, u32[]{:S(2)}, u32[]{:S(2)}) collective-permute-start(bf16[768,512]{1,0:T(8,128)(2,1)S(1)} %get-tuple-element.116.refs_3_.refs_0_), channel_id=1, source_target_pairs={{1,2},{2,1},{5,6},{6,5},{9,10},{10,9},{13,14},{14,13},{17,18},{18,... | collective-permute-start | bytes 2359304 | tf_op jit(solution)/shard_map/ppermute | solution.py:415
  32.8 31.2 %collective-permute-start.6 = (bf16[768,512]{1,0:T(8,128)(2,1)S(1)}, bf16[768,512]{1,0:T(8,128)(2,1)S(1)}, u32[]{:S(2)}, u32[]{:S(2)}) collective-permute-start(bf16[768,512]{1,0:T(8,128)(2,1)S(1)} %get-tuple-element.114), channel_id=1, source_target_pairs={{0,1},{1,0},{2,3},{3,2},{4,5},{5,4},{6,7},{7,6},{8,9},{9,8},{10,11... | collective-permute-start | bytes 2359304 | tf_op jit(solution)/shard_map/ppermute | solution.py:415
  48.0 17.5 %collective-permute-start.5 = (bf16[768,512]{1,0:T(8,128)(2,1)S(1)}, bf16[768,512]{1,0:T(8,128)(2,1)S(1)}, u32[]{:S(2)}, u32[]{:S(2)}) collective-permute-start(bf16[768,512]{1,0:T(8,128)(2,1)S(1)} %get-tuple-element.111), channel_id=1, source_target_pairs={{1,2},{2,1},{5,6},{6,5},{9,10},{10,9},{13,14},{14,13},{17,18},{18,... | collective-permute-start | bytes 2359304 | tf_op jit(solution)/shard_map/ppermute | solution.py:415
  48.7 32.2 %collective-permute-start.10 = (bf16[768,512]{1,0:T(8,128)(2,1)S(1)}, bf16[768,512]{1,0:T(8,128)(2,1)S(1)}, u32[]{:S(2)}, u32[]{:S(2)}) collective-permute-start(bf16[768,512]{1,0:T(8,128)(2,1)S(1)} %get-tuple-element.123), channel_id=1, source_target_pairs={{0,1},{1,0},{2,3},{3,2},{4,5},{5,4},{6,7},{7,6},{8,9},{9,8},{10,11... | collective-permute-start | bytes 2359304 | tf_op jit(solution)/shard_map/ppermute | solution.py:415
  65.4 34.1 %collective-permute-start.9 = (bf16[768,512]{1,0:T(8,128)(2,1)S(1)}, bf16[768,512]{1,0:T(8,128)(2,1)S(1)}, u32[]{:S(2)}, u32[]{:S(2)}) collective-permute-start(bf16[768,512]{1,0:T(8,128)(2,1)S(1)} %get-tuple-element.122), channel_id=1, source_target_pairs={{1,2},{2,1},{5,6},{6,5},{9,10},{10,9},{13,14},{14,13},{17,18},{18,... | collective-permute-start | bytes 2359304 | tf_op jit(solution)/shard_map/ppermute | solution.py:415
  66.2 35.4 %collective-permute-start.8 = (bf16[768,512]{1,0:T(8,128)(2,1)S(1)}, bf16[768,512]{1,0:T(8,128)(2,1)S(1)}, u32[]{:S(2)}, u32[]{:S(2)}) collective-permute-start(bf16[768,512]{1,0:T(8,128)(2,1)S(1)} %get-tuple-element.121.refs_1_), channel_id=1, source_target_pairs={{0,1},{1,0},{2,3},{3,2},{4,5},{5,4},{6,7},{7,6},{8,9},{9,8},{10,11... | collective-permute-start | bytes 2359304 | tf_op jit(solution)/shard_map/ppermute | solution.py:415
  81.7 32.1 %collective-permute-start.12 = (bf16[768,512]{1,0:T(8,128)(2,1)S(1)}, bf16[768,512]{1,0:T(8,128)(2,1)S(1)}, u32[]{:S(2)}, u32[]{:S(2)}) collective-permute-start(bf16[768,512]{1,0:T(8,128)(2,1)S(1)} %get-tuple-element.130), channel_id=1, source_target_pairs={{1,2},{2,1},{5,6},{6,5},{9,10},{10,9},{13,14},{14,13},{17,18},{18,... | collective-permute-start | bytes 2359304 | tf_op jit(solution)/shard_map/ppermute | solution.py:415
  81.8 26.1 %collective-permute-start.13 = (bf16[192,1024]{1,0:T(8,128)(2,1)S(1)}, bf16[192,1024]{1,0:T(8,128)(2,1)S(1)}, u32[]{:S(2)}, u32[]{:S(2)}) collective-permute-start(bf16[192,1024]{1,0:T(8,128)(2,1)S(1)} %get-tuple-element.132.refs_0_), channel_id=1, source_target_pairs={{0,1},{1,0},{2,3},{3,2},{4,5},{5,4},{6,7},{7,6},{8,9},{9,8},{10,11... | collective-permute-start | bytes 1179656 | tf_op jit(solution)/shard_map/ppermute | solution.py:415
  94.1 14.6 %slice-start.2 = ((s8[4718592]{0:T(1024)(128)(4,1)}), s8[4194304]{0:T(1024)(128)(4,1)S(1)}, s32[]{:S(2)}) async-start(s8[4718592]{0:T(1024)(128)(4,1)} %bitcast.8), calls=%async_computation.2 | async-start | bytes 8388608
  100.2 22.8 %collective-permute-start.11 = (bf16[768,512]{1,0:T(8,128)(2,1)S(1)}, bf16[768,512]{1,0:T(8,128)(2,1)S(1)}, u32[]{:S(2)}, u32[]{:S(2)}) collective-permute-start(bf16[768,512]{1,0:T(8,128)(2,1)S(1)} %get-tuple-element.129.refs_1_.refs_3_), channel_id=1, source_target_pairs={{0,1},{1,0},{2,3},{3,2},{4,5},{5,4},{6,7},{7,6},{8,9},{9,8},{10,11... | collective-permute-start | bytes 2359304 | tf_op jit(solution)/shard_map/ppermute | solution.py:415
  102.3 32.0 %collective-permute-start.15 = (bf16[768,512]{1,0:T(8,128)(2,1)S(1)}, bf16[768,512]{1,0:T(8,128)(2,1)S(1)}, u32[]{:S(2)}, u32[]{:S(2)}) collective-permute-start(bf16[768,512]{1,0:T(8,128)(2,1)S(1)} %get-tuple-element.140), channel_id=1, source_target_pairs={{1,2},{2,1},{5,6},{6,5},{9,10},{10,9},{13,14},{14,13},{17,18},{18,... | collective-permute-start | bytes 2359304 | tf_op jit(solution)/shard_map/ppermute | solution.py:415
  102.4 6.3 %slice-start.3 = ((s8[4718592]{0:T(1024)(128)(4,1)}), s8[524288]{0:T(1024)(128)(4,1)S(1)}, s32[]{:S(2)}) async-start(s8[4718592]{0:T(1024)(128)(4,1)} %bitcast.8), calls=%async_computation.3 | async-start | bytes 1048576
  114.4 26.4 %collective-permute-start.14 = (bf16[768,512]{1,0:T(8,128)(2,1)S(1)}, bf16[768,512]{1,0:T(8,128)(2,1)S(1)}, u32[]{:S(2)}, u32[]{:S(2)}) collective-permute-start(bf16[768,512]{1,0:T(8,128)(2,1)S(1)} %get-tuple-element.139.refs_1_.refs_5_), channel_id=1, source_target_pairs={{0,1},{1,0},{2,3},{3,2},{4,5},{5,4},{6,7},{7,6},{8,9},{9,8},{10,11... | collective-permute-start | bytes 2359304 | tf_op jit(solution)/shard_map/ppermute | solution.py:415
  116.5 25.1 %collective-permute-start.18 = (bf16[768,512]{1,0:T(8,128)(2,1)S(1)}, bf16[768,512]{1,0:T(8,128)(2,1)S(1)}, u32[]{:S(2)}, u32[]{:S(2)}) collective-permute-start(bf16[768,512]{1,0:T(8,128)(2,1)S(1)} %get-tuple-element.150.refs_3_.refs_0_), channel_id=1, source_target_pairs={{1,2},{2,1},{5,6},{6,5},{9,10},{10,9},{13,14},{14,13},{17,18},{18,... | collective-permute-start | bytes 2359304 | tf_op jit(solution)/shard_map/ppermute | solution.py:415
  123.8 17.8 %collective-permute-start.19 = (bf16[768,512]{1,0:T(8,128)(2,1)S(1)}, bf16[768,512]{1,0:T(8,128)(2,1)S(1)}, u32[]{:S(2)}, u32[]{:S(2)}) collective-permute-start(bf16[768,512]{1,0:T(8,128)(2,1)S(1)} %get-tuple-element.152), channel_id=1, source_target_pairs={{1,2},{2,1},{5,6},{6,5},{9,10},{10,9},{13,14},{14,13},{17,18},{18,... | collective-permute-start | bytes 2359304 | tf_op jit(solution)/shard_map/ppermute | solution.py:415
  135.0 32.3 %collective-permute-start.16 = (bf16[768,512]{1,0:T(8,128)(2,1)S(1)}, bf16[768,512]{1,0:T(8,128)(2,1)S(1)}, u32[]{:S(2)}, u32[]{:S(2)}) collective-permute-start(bf16[768,512]{1,0:T(8,128)(2,1)S(1)} %get-tuple-element.147.refs_1_.refs_7_), channel_id=1, source_target_pairs={{0,1},{1,0},{2,3},{3,2},{4,5},{5,4},{6,7},{7,6},{8,9},{9,8},{10,11... | collective-permute-start | bytes 2359304 | tf_op jit(solution)/shard_map/ppermute | solution.py:415
  141.6 31.1 %collective-permute-start.17 = (bf16[768,512]{1,0:T(8,128)(2,1)S(1)}, bf16[768,512]{1,0:T(8,128)(2,1)S(1)}, u32[]{:S(2)}, u32[]{:S(2)}) collective-permute-start(bf16[768,512]{1,0:T(8,128)(2,1)S(1)} %get-tuple-element.149), channel_id=1, source_target_pairs={{1,2},{2,1},{5,6},{6,5},{9,10},{10,9},{13,14},{14,13},{17,18},{18,... | collective-permute-start | bytes 2359304 | tf_op jit(solution)/shard_map/ppermute | solution.py:415
  142.3 50.5 %collective-permute-start.20 = (bf16[768,512]{1,0:T(8,128)(2,1)S(1)}, bf16[768,512]{1,0:T(8,128)(2,1)S(1)}, u32[]{:S(2)}, u32[]{:S(2)}) collective-permute-start(bf16[768,512]{1,0:T(8,128)(2,1)S(1)} %get-tuple-element.162.refs_2_.refs_1_), channel_id=1, source_target_pairs={{0,1},{1,0},{2,3},{3,2},{4,5},{5,4},{6,7},{7,6},{8,9},{9,8},{10,11... | collective-permute-start | bytes 2359304 | tf_op jit(solution)/shard_map/ppermute | solution.py:415
  173.3 19.5 %collective-permute-start.21 = (bf16[768,512]{1,0:T(8,128)(2,1)S(1)}, bf16[768,512]{1,0:T(8,128)(2,1)S(1)}, u32[]{:S(2)}, u32[]{:S(2)}) collective-permute-start(bf16[768,512]{1,0:T(8,128)(2,1)S(1)} %get-tuple-element.163.refs_4_.refs_1_), channel_id=1, source_target_pairs={{0,1},{1,0},{2,3},{3,2},{4,5},{5,4},{6,7},{7,6},{8,9},{9,8},{10,11... | collective-permute-start | bytes 2359304 | tf_op jit(solution)/shard_map/ppermute | solution.py:415
  188.6 3.7 %copy-start.4 = (f32[768,3072]{1,0:T(8,128)}, f32[768,3072]{1,0:T(8,128)S(1)}, u32[]{:S(2)}) copy-start(f32[768,3072]{1,0:T(8,128)S(1)} %get-tuple-element.161.refs_1_) | copy-start | bytes 28311556
  203.8 1.4 copy-start.5
  205.1 4.7 %collective-permute-start.22 = (bf16[384,3072]{1,0:T(8,128)(2,1)}, bf16[384,3072]{1,0:T(8,128)(2,1)S(1)}, u32[]{:S(2)}, u32[]{:S(2)}) collective-permute-start(bf16[384,3072]{1,0:T(8,128)(2,1)} %copy-done.5), channel_id=1, source_target_pairs={{0,4},{4,0},{8,12},{12,8},{16,20},{20,16},{24,28},{28,24},{1,5},{5... | collective-permute-start | bytes 7077896 | tf_op jit(solution)/shard_map/ppermute | solution.py:419
  205.2 21.6 %collective-permute-start.25 = (bf16[768,512]{1,0:T(8,128)(2,1)S(1)}, bf16[768,512]{1,0:T(8,128)(2,1)S(1)}, u32[]{:S(2)}, u32[]{:S(2)}) collective-permute-start(bf16[768,512]{1,0:T(8,128)(2,1)S(1)} %get-tuple-element.173.refs_1_), channel_id=1, source_target_pairs={{0,1},{1,0},{2,3},{3,2},{4,5},{5,4},{6,7},{7,6},{8,9},{9,8},{10,11... | collective-permute-start | bytes 2359304 | tf_op jit(solution)/shard_map/ppermute | solution.py:415
  211.4 20.8 %collective-permute-start.23 = (bf16[192,1536]{1,0:T(8,128)(2,1)S(1)}, bf16[192,1536]{1,0:T(8,128)(2,1)S(1)}, u32[]{:S(2)}, u32[]{:S(2)}) collective-permute-start(bf16[192,1536]{1,0:T(8,128)(2,1)S(1)} %get-tuple-element.170), channel_id=1, source_target_pairs={{0,8},{4,12},{8,0},{12,4},{16,24},{20,28},{24,16},{28,20},{1,9},{5... | collective-permute-start | bytes 1769480 | tf_op jit(solution)/shard_map/ppermute | solution.py:419
  212.9 19.3 %collective-permute-start.24 = (bf16[192,1536]{1,0:T(8,128)(2,1)S(1)}, bf16[192,1536]{1,0:T(8,128)(2,1)S(1)}, u32[]{:S(2)}, u32[]{:S(2)}) collective-permute-start(bf16[192,1536]{1,0:T(8,128)(2,1)S(1)} %get-tuple-element.172), channel_id=1, source_target_pairs={{0,16},{4,20},{8,24},{12,28},{16,0},{20,4},{24,8},{28,12},{1,17},{... | collective-permute-start | bytes 1769480 | tf_op jit(solution)/shard_map/ppermute | solution.py:419
  214.4 2.3 copy-start.1
  233.0 8.6 %collective-permute-start.26 = (bf16[96,1536]{1,0:T(8,128)(2,1)S(1)}, bf16[96,1536]{1,0:T(8,128)(2,1)S(1)}, u32[]{:S(2)}, u32[]{:S(2)}) collective-permute-start(bf16[96,1536]{1,0:T(8,128)(2,1)S(1)} %get-tuple-element.182), channel_id=1, source_target_pairs={{0,16},{4,20},{8,24},{12,28},{16,0},{20,4},{24,8},{28,12},{1,17},{... | collective-permute-start | bytes 884744 | tf_op jit(solution)/shard_map/ppermute | solution.py:419
  233.6 8.2 %collective-permute-start.27 = (bf16[96,1536]{1,0:T(8,128)(2,1)S(1)}, bf16[96,1536]{1,0:T(8,128)(2,1)S(1)}, u32[]{:S(2)}, u32[]{:S(2)}) collective-permute-start(bf16[96,1536]{1,0:T(8,128)(2,1)S(1)} %get-tuple-element.184), channel_id=1, source_target_pairs={{0,8},{4,12},{8,0},{12,4},{16,24},{20,28},{24,16},{28,20},{1,9},{5... | collective-permute-start | bytes 884744 | tf_op jit(solution)/shard_map/ppermute | solution.py:419

commit v3 on v2

--- a/solution.py
+++ b/solution.py
@@ -299,7 +299,7 @@
         [pl.BlockSpec((bd, width), lambda i, s: (i, start // width))] + [whole(*part.shape) for part in flat],
         [pl.BlockSpec((tokens, bd), lambda i, s: (0, i))],
         [shape32(tokens, model)], [w_in] + flat, after,
-        scratch=[pltpu.VMEM((tokens, width), jnp.bfloat16)],
+        scratch=[pltpu.VMEM((tokens, width), jnp.bfloat16)], vmem=LARGE,
     )
 
 
@@ -406,7 +406,7 @@
 WITH = {"I0": 1, "I1": 2, "C0": 3, "C1": 4, "C2": 5}
 ORDER = (
     "O0", "O1", "A0", "N0", "A2", "Q0", "N1", "I0", "B0", "I1", "B1", "O2", "C0", "B2", "A4", "V0", "C1", "B3", "V1",
-    "N2", "W0", "C2", "B4", "W1", "V2", "C3", "B5", "C4", "W2", "V3", "W3", "C5", "T0", "I2", "T1", "R1", "W4", "W5",
+    "N2", "W0", "C2", "B4", "W1", "V2", "C3", "B5", "W2", "V3", "C4", "T0", "C5", "W3", "I2", "W4", "T1", "R1", "W5",
     "V4", "R2", "V5", "R3",
 )
 

time: 247 us -> 255 us (1.032)
  Pallas kernels: 131 us -> 139 us
  starting transfers between devices: 57.2 us -> 52.4 us
  local copies, waits for them, and re-layouts: 11.1 us -> 14 us
    pallas_call x42, Pallas kernels: 131 us -> 139 us  [call(): pl.pallas_call(kernel, grid_spec=pltpu.PrefetchScalarGridSpec(num_scalar_...]
    ppermute x23, starting transfers between devices: 52.8 us -> 46.3 us  [send(): return lax.ppermute(value, ('row', 'col'), perm)]
    unnamed x20 -> x62, local copies, waits for them, and re-layouts: 11 us -> 14 us
  transfers between devices with their start and end apart: 28 -> 28, of which waited for: 7 -> 9; matrix products, arithmetic and copies ran while one was open for 0% -> 0% of each run, Pallas kernels for 48% -> 50%
where the time goes in v3:
time: 255 us; the launch traced here: 251 us
  Pallas kernels  139 us (55%)
  starting transfers between devices  52.4 us (21%)
  waiting for transfers between devices  44.3 us (17%)
  local copies, waits for them, and re-layouts  14 us (5%)
    pallas_call x42, Pallas kernels, call(): pl.pallas_call(kernel, grid_spec=pltpu.PrefetchScalarGridSpec(num_scalar_...  139 us
    ppermute x23, starting transfers between devices, send(): return lax.ppermute(value, ('row', 'col'), perm)  46.3 us
    ppermute x23, waiting for transfers between devices, send(): return lax.ppermute(value, ('row', 'col'), perm)  39.8 us
    unnamed x62, local copies, waits for them, and re-layouts  14 us
    ppermute x5, starting transfers between devices, swap(): return lax.ppermute(value, 'row', [(i, i ^ bit) for i in range(ROW)])  6.11 us
  transfers between devices with their start and end apart: 28, of which 9 were waited for; matrix products, arithmetic and copies ran while one was open for 0% of the time, Pallas kernels for 50%

profile of v3, /device:TPU:0, one launch (start us, length us, event | category | flops | bytes accessed | tf_op | source)
XLA Modules:
  0.0 251.0 jit_solution(15872616085810601183)
XLA Ops:
  0.8 1.3 copy-done.2
  2.6 3.1 %collective-permute-start.1 = (bf16[192,1024]{1,0:T(8,128)(2,1)S(1)}, bf16[192,1024]{1,0:T(8,128)(2,1)S(1)}, u32[]{:S(2)}, u32[]{:S(2)}) collective-permute-start(bf16[192,1024]{1,0:T(8,128)(2,1)S(1)} %get-tuple-element.101.refs_0_), channel_id=1, source_target_pairs={{0,1},{1,0},{2,3},{3,2},{4,5},{5,4},{6,7},{7,6},{8,9},{9,8},{10,11... | collective-permute-start | bytes 1179656 | tf_op jit(solution)/shard_map/ppermute | solution.py:415
  6.3 2.3 copy-done
  8.6 8.2 %shard_map.78 = (bf16[768,512]{1,0:T(8,128)(2,1)S(1)}, bf16[768,512]{1,0:T(8,128)(2,1)S(1)}, f32[8,128]{1,0:T(8,128)S(1)}) custom-call(s32[6]{0:T(128)S(1)} %stack.31.place_ref, bf16[768,3072]{1,0:T(8,128)(2,1)S(1)} %copy-done, bf16[3072,3072]{1,0:T(8,128)(2,1)} %refs_1_.5, f32[8,128]{1,0:T(8,128)S(1)} %get-tuple-element.98.refs_2_), custom_call_target="tpu_custom_call" | custom-call | tf_op jit(solution)/shard_map/pallas_call | solution.py:45
  18.1 2.7 %collective-permute-start.4 = (bf16[192,1024]{1,0:T(8,128)(2,1)S(1)}, bf16[192,1024]{1,0:T(8,128)(2,1)S(1)}, u32[]{:S(2)}, u32[]{:S(2)}) collective-permute-start(bf16[192,1024]{1,0:T(8,128)(2,1)S(1)} %get-tuple-element.107.refs_0_), channel_id=1, source_target_pairs={{0,1},{1,0},{2,3},{3,2},{4,5},{5,4},{6,7},{7,6},{8,9},{9,8},{10,11... | collective-permute-start | bytes 1179656 | tf_op jit(solution)/shard_map/ppermute | solution.py:415
  20.8 2.0 collective-permute-start
  22.8 7.9 %shard_map.80 = (bf16[768,512]{1,0:T(8,128)(2,1)S(1)}, bf16[768,512]{1,0:T(8,128)(2,1)S(1)}, f32[8,128]{1,0:T(8,128)S(1)}) custom-call(s32[6]{0:T(128)S(1)} %stack.31.place_ref, bf16[768,3072]{1,0:T(8,128)(2,1)S(1)} %bitcast.7, bf16[3072,3072]{1,0:T(8,128)(2,1)} %refs_1_.5, f32[8,128]{1,0:T(8,128)S(1)} %get-tuple-element.104.refs_2_), custom_call_target="tpu_custom_call" | custom-call | tf_op jit(solution)/shard_map/pallas_call | solution.py:45
  31.3 0.8 shard_map.82
  32.9 3.5 %collective-permute-start.6 = (bf16[768,512]{1,0:T(8,128)(2,1)S(1)}, bf16[768,512]{1,0:T(8,128)(2,1)S(1)}, u32[]{:S(2)}, u32[]{:S(2)}) collective-permute-start(bf16[768,512]{1,0:T(8,128)(2,1)S(1)} %get-tuple-element.114), channel_id=1, source_target_pairs={{0,1},{1,0},{2,3},{3,2},{4,5},{5,4},{6,7},{7,6},{8,9},{9,8},{10,11... | collective-permute-start | bytes 2359304 | tf_op jit(solution)/shard_map/ppermute | solution.py:415
  36.4 10.9 %collective-permute-done.refs_1_ = bf16[768,512]{1,0:T(8,128)(2,1)S(1)} collective-permute-done((bf16[768,512]{1,0:T(8,128)(2,1)S(1)}, bf16[768,512]{1,0:T(8,128)(2,1)S(1)}, u32[]{:S(2)}, u32[]{:S(2)}) %collective-permute-start) | collective-permute-done | bytes 786464 | tf_op jit(solution)/shard_map/ppermute | solution.py:415
  47.2 0.8 shard_map.84
  48.8 4.5 %collective-permute-start.10 = (bf16[768,512]{1,0:T(8,128)(2,1)S(1)}, bf16[768,512]{1,0:T(8,128)(2,1)S(1)}, u32[]{:S(2)}, u32[]{:S(2)}) collective-permute-start(bf16[768,512]{1,0:T(8,128)(2,1)S(1)} %get-tuple-element.123), channel_id=1, source_target_pairs={{0,1},{1,0},{2,3},{3,2},{4,5},{5,4},{6,7},{7,6},{8,9},{9,8},{10,11... | collective-permute-start | bytes 2359304 | tf_op jit(solution)/shard_map/ppermute | solution.py:415
  53.2 10.8 %collective-permute-done.6.refs_1_.refs_2_ = bf16[768,512]{1,0:T(8,128)(2,1)S(1)} collective-permute-done((bf16[768,512]{1,0:T(8,128)(2,1)S(1)}, bf16[768,512]{1,0:T(8,128)(2,1)S(1)}, u32[]{:S(2)}, u32[]{:S(2)}) %collective-permute-start.6) | collective-permute-done | bytes 786464 | tf_op jit(solution)/shard_map/ppermute | solution.py:415
  64.1 1.5 shard_map.86
  66.3 1.5 shard_map.88
  67.8 5.6 %collective-permute-start.8 = (bf16[768,512]{1,0:T(8,128)(2,1)}, bf16[768,512]{1,0:T(8,128)(2,1)S(1)}, u32[]{:S(2)}, u32[]{:S(2)}) collective-permute-start(bf16[768,512]{1,0:T(8,128)(2,1)} %get-tuple-element.121.refs_1_), channel_id=1, source_target_pairs={{0,1},{1,0},{2,3},{3,2},{4,5},{5,4},{6,7},{7,6},{8,9},{9,8},{10,11... | collective-permute-start | bytes 2359304 | tf_op jit(solution)/shard_map/ppermute | solution.py:415
  73.3 7.6 %collective-permute-done.10.refs_1_.refs_2_ = bf16[768,512]{1,0:T(8,128)(2,1)S(1)} collective-permute-done((bf16[768,512]{1,0:T(8,128)(2,1)S(1)}, bf16[768,512]{1,0:T(8,128)(2,1)S(1)}, u32[]{:S(2)}, u32[]{:S(2)}) %collective-permute-start.10) | collective-permute-done | bytes 786464 | tf_op jit(solution)/shard_map/ppermute | solution.py:415
  80.9 1.6 shard_map.89
  82.5 4.4 %collective-permute-start.13 = (bf16[192,1024]{1,0:T(8,128)(2,1)S(1)}, bf16[192,1024]{1,0:T(8,128)(2,1)S(1)}, u32[]{:S(2)}, u32[]{:S(2)}) collective-permute-start(bf16[192,1024]{1,0:T(8,128)(2,1)S(1)} %get-tuple-element.132.refs_0_), channel_id=1, source_target_pairs={{0,1},{1,0},{2,3},{3,2},{4,5},{5,4},{6,7},{7,6},{8,9},{9,8},{10,11... | collective-permute-start | bytes 1179656 | tf_op jit(solution)/shard_map/ppermute | solution.py:415
  86.9 7.9 %shard_map.90 = (bf16[768,512]{1,0:T(8,128)(2,1)S(1)}, bf16[768,512]{1,0:T(8,128)(2,1)S(1)}, f32[8,128]{1,0:T(8,128)S(1)}) custom-call(s32[6]{0:T(128)S(1)} %stack.31.place_ref, bf16[768,3072]{1,0:T(8,128)(2,1)S(1)} %bitcast.7, bf16[3072,3072]{1,0:T(8,128)(2,1)} %refs_1_.5, f32[8,128]{1,0:T(8,128)S(1)} %get-tuple-element.125.refs_2_), custom_call_target="tpu_custom_call" | custom-call | tf_op jit(solution)/shard_map/pallas_call | solution.py:45
  94.8 5.5 %shard_map.91 = (bf16[3072,3072]{1,0:T(8,128)(2,1)}, f32[8,128]{1,0:T(8,128)S(1)}) custom-call(s32[6]{0:T(128)S(1)} %stack.31.place_ref, bf16[768,512]{1,0:T(8,128)(2,1)S(1)} %get-tuple-element.112.refs_3_.refs_0_, bf16[768,512]{1,0:T(8,128)(2,1)S(1)} %get-tuple-element.106.refs_1_.refs_4_, bf16[768,512]{1,0:T(8,128)(2,1)S(1)} %collective-permute-done.6.refs_1_.refs_2_, ...), custom_call_target="tpu_custom_call" | custom-call | tf_op jit(solution)/shard_map/pallas_call | solution.py:45
  100.3 0.9 copy-done.24
  101.2 1.1 copy-done.11
  102.3 1.1 copy-done.25
  104.1 1.3 collective-permute-start.11
  106.3 5.5 %shard_map.94 = (bf16[3072,3072]{1,0:T(8,128)(2,1)}, f32[8,128]{1,0:T(8,128)S(1)}) custom-call(s32[6]{0:T(128)S(1)} %stack.31.place_ref, bf16[768,512]{1,0:T(8,128)(2,1)S(1)} %get-tuple-element.112.refs_3_.refs_0_, bf16[768,512]{1,0:T(8,128)(2,1)S(1)} %get-tuple-element.106.refs_1_.refs_4_, ...), custom_call_target="tpu_custom_call", output_to_operand_aliasing={{0}: (5, {})} | custom-call | tf_op jit(solution)/shard_map/pallas_call | solution.py:45
  111.8 0.8 shard_map.95
  112.7 6.0 %shard_map.96 = (bf16[3072,3072]{1,0:T(8,128)(2,1)}, f32[8,128]{1,0:T(8,128)S(1)}) custom-call(s32[6]{0:T(128)S(1)} %stack.31.place_ref, bf16[768,3072]{1,0:T(8,128)(2,1)S(1)} %bitcast.9, bf16[768,512]{1,0:T(8,128)(2,1)} %get-tuple-element.121.refs_1_, bf16[768,512]{1,0:T(8,128)(2,1)S(1)} %collective-permute-done.8.refs_1_.refs_2_, ...), custom_call_target="tpu_custom_call" | custom-call | tf_op jit(solution)/shard_map/pallas_call | solution.py:45
  118.7 1.7 shard_map.97
  120.4 2.1 collective-permute-start.14
  123.9 5.0 %shard_map.99 = (bf16[3072,3072]{1,0:T(8,128)(2,1)}, f32[8,128]{1,0:T(8,128)S(1)}) custom-call(s32[6]{0:T(128)S(1)} %stack.31.place_ref, bf16[768,3072]{1,0:T(8,128)(2,1)S(1)} %bitcast.9, bf16[768,512]{1,0:T(8,128)(2,1)S(1)} %get-tuple-element.129.refs_1_.refs_3_, ...), custom_call_target="tpu_custom_call", output_to_operand_aliasing={{0}: (4, {})} | custom-call | tf_op jit(solution)/shard_map/pallas_call | solution.py:45
  128.8 5.5 %shard_map.100 = (bf16[3072,3072]{1,0:T(8,128)(2,1)}, f32[8,128]{1,0:T(8,128)S(1)}) custom-call(s32[6]{0:T(128)S(1)} %stack.31.place_ref, bf16[768,512]{1,0:T(8,128)(2,1)S(1)} %get-tuple-element.116.refs_3_.refs_0_, bf16[768,512]{1,0:T(8,128)(2,1)S(1)} %collective-permute-done.7.refs_1_.refs_4_, ...), custom_call_target="tpu_custom_call", output_to_operand_aliasing={{0}: (5, {})} | custom-call | tf_op jit(solution)/shard_map/pallas_call | solution.py:45
  135.0 4.4 %collective-permute-start.16 = (bf16[768,512]{1,0:T(8,128)(2,1)S(1)}, bf16[768,512]{1,0:T(8,128)(2,1)S(1)}, u32[]{:S(2)}, u32[]{:S(2)}) collective-permute-start(bf16[768,512]{1,0:T(8,128)(2,1)S(1)} %get-tuple-element.147.refs_7_.refs_1_), channel_id=1, source_target_pairs={{0,1},{1,0},{2,3},{3,2},{4,5},{5,4},{6,7},{7,6},{8,9},{9,8},{10,11... | collective-permute-start | bytes 2359304 | tf_op jit(solution)/shard_map/ppermute | solution.py:415
  139.4 1.4 collective-permute-done.14.refs_1_.refs_2_.refs_6_
  140.8 1.6 shard_map.102
  142.4 5.0 %shard_map.103 = (bf16[3072,3072]{1,0:T(8,128)(2,1)}, f32[8,128]{1,0:T(8,128)S(1)}) custom-call(s32[6]{0:T(128)S(1)} %stack.31.place_ref, bf16[768,3072]{1,0:T(8,128)(2,1)S(1)} %bitcast.9, bf16[768,512]{1,0:T(8,128)(2,1)S(1)} %get-tuple-element.139.refs_1_.refs_5_, ...), custom_call_target="tpu_custom_call", output_to_operand_aliasing={{0}: (4, {})} | custom-call | tf_op jit(solution)/shard_map/pallas_call | solution.py:45
  147.4 5.5 %shard_map.104 = (bf16[3072,3072]{1,0:T(8,128)(2,1)}, f32[8,128]{1,0:T(8,128)S(1)}) custom-call(s32[6]{0:T(128)S(1)} %stack.31.place_ref, bf16[768,512]{1,0:T(8,128)(2,1)S(1)} %get-tuple-element.116.refs_3_.refs_0_, bf16[768,512]{1,0:T(8,128)(2,1)S(1)} %collective-permute-done.7.refs_1_.refs_4_, ...), custom_call_target="tpu_custom_call", output_to_operand_aliasing={{0}: (5, {})} | custom-call | tf_op jit(solution)/shard_map/pallas_call | solution.py:45
  153.6 8.2 %collective-permute-start.19 = (bf16[768,512]{1,0:T(8,128)(2,1)S(1)}, bf16[768,512]{1,0:T(8,128)(2,1)S(1)}, u32[]{:S(2)}, u32[]{:S(2)}) collective-permute-start(bf16[768,512]{1,0:T(8,128)(2,1)S(1)} %get-tuple-element.158.refs_1_.refs_2_), channel_id=1, source_target_pairs={{0,1},{1,0},{2,3},{3,2},{4,5},{5,4},{6,7},{7,6},{8,9},{9,8},{10,11... | collective-permute-start | bytes 2359304 | tf_op jit(solution)/shard_map/ppermute | solution.py:415
  161.8 1.1 copy-done.19
  163.0 15.9 %shard_map.106 = (f32[768,3072]{1,0:T(8,128)}, f32[8,128]{1,0:T(8,128)S(1)}) custom-call(s32[6]{0:T(128)S(1)} %stack.31.place_ref, bf16[3072,3072]{1,0:T(8,128)(2,1)} %refs_0_.26, bf16[768,512]{1,0:T(8,128)(2,1)} %get-tuple-element.121.refs_1_, bf16[768,512]{1,0:T(8,128)(2,1)S(1)} %collective-permute-done.8.refs_1_.refs_2_, bf16[768,512]{1,0:T(8,128)(2,1)S(1)} %copy-done.15, ...), custom_call_target="tpu_custom_call" | custom-call | tf_op jit(solution)/shard_map/pallas_call | solution.py:45
  178.9 1.7 shard_map.107
  180.6 1.5 collective-permute-start.21
  182.1 5.0 %shard_map.108 = (bf16[3072,3072]{1,0:T(8,128)(2,1)}, f32[8,128]{1,0:T(8,128)S(1)}) custom-call(s32[6]{0:T(128)S(1)} %stack.31.place_ref, bf16[768,3072]{1,0:T(8,128)(2,1)S(1)} %bitcast.9, bf16[768,512]{1,0:T(8,128)(2,1)S(1)} %copy-done.19, bf16[768,512]{1,0:T(8,128)(2,1)S(1)} %collective-permute-done.16.refs_8_.refs_2_, ...), custom_call_target="tpu_custom_call", output_to_operand_aliasing={{0}: (4, {})} | custom-call | tf_op jit(solution)/shard_map/pallas_call | solution.py:45
  187.6 5.0 %shard_map.110 = (bf16[3072,3072]{1,0:T(8,128)(2,1)}, f32[8,128]{1,0:T(8,128)S(1)}) custom-call(s32[6]{0:T(128)S(1)} %stack.31.place_ref, bf16[768,3072]{1,0:T(8,128)(2,1)S(1)} %bitcast.9, bf16[768,512]{1,0:T(8,128)(2,1)S(1)} %get-tuple-element.158.refs_1_.refs_2_, ...), custom_call_target="tpu_custom_call", output_to_operand_aliasing={{0}: (4, {})} | custom-call | tf_op jit(solution)/shard_map/pallas_call | solution.py:45
  192.6 5.7 %collective-permute-done.21.refs_5_.refs_2_ = bf16[768,512]{1,0:T(8,128)(2,1)S(1)} collective-permute-done((bf16[768,512]{1,0:T(8,128)(2,1)S(1)}, bf16[768,512]{1,0:T(8,128)(2,1)S(1)}, u32[]{:S(2)}, u32[]{:S(2)}) %collective-permute-start.21) | collective-permute-done | bytes 786464 | tf_op jit(solution)/shard_map/ppermute | solution.py:415
  198.4 1.1 copy-done.21
  199.5 1.1 copy-done.23
  200.6 10.9 %shard_map.111 = (f32[384,3072]{1,0:T(8,128)S(1)}, bf16[384,3072]{1,0:T(8,128)(2,1)S(1)}, f32[8,128]{1,0:T(8,128)S(1)}) custom-call(s32[6]{0:T(128)S(1)} %stack.31.place_ref, bf16[3072,3072]{1,0:T(8,128)(2,1)} %refs_0_.26, f32[768,3072]{1,0:T(8,128)} %get-tuple-element.157.refs_1_, bf16[768,512]{1,0:T(8,128)(2,1)S(1)} %copy-done.21, ...), custom_call_target="tpu_custom_call" | custom-call | tf_op jit(solution)/shard_map/pallas_call | solution.py:45
  211.6 1.4 copy-done.26
  212.9 1.7 collective-permute-start.25
  214.6 3.1 %collective-permute-done.22.refs_1_ = bf16[384,3072]{1,0:T(8,128)(2,1)S(1)} collective-permute-done((bf16[384,3072]{1,0:T(8,128)(2,1)}, bf16[384,3072]{1,0:T(8,128)(2,1)S(1)}, u32[]{:S(2)}, u32[]{:S(2)}) %collective-permute-start.22) | collective-permute-done | bytes 2359328 | tf_op jit(solution)/shard_map/ppermute | solution.py:419
  217.7 1.5 shard_map.112
  219.2 1.6 collective-permute-start.23
  220.7 1.5 collective-permute-start.24
  222.2 2.3 copy-done.1
  224.6 5.0 %shard_map.113 = (bf16[3072,3072]{1,0:T(8,128)(2,1)}, f32[8,128]{1,0:T(8,128)S(1)}) custom-call(s32[6]{0:T(128)S(1)} %stack.31.place_ref, bf16[768,3072]{1,0:T(8,128)(2,1)S(1)} %copy-done.1, bf16[768,512]{1,0:T(8,128)(2,1)S(1)} %get-tuple-element.161.refs_4_.refs_1_, ...), custom_call_target="tpu_custom_call", output_to_operand_aliasing={{0}: (4, {})} | custom-call | tf_op jit(solution)/shard_map/pallas_call | solution.py:45
  229.5 3.3 %collective-permute-done.25.refs_2_ = bf16[768,512]{1,0:T(8,128)(2,1)S(1)} collective-permute-done((bf16[768,512]{1,0:T(8,128)(2,1)S(1)}, bf16[768,512]{1,0:T(8,128)(2,1)S(1)}, u32[]{:S(2)}, u32[]{:S(2)}) %collective-permute-start.25) | collective-permute-done | bytes 786464 | tf_op jit(solution)/shard_map/ppermute | solution.py:415
  232.9 5.5 %shard_map.114 = (bf16[3072,3072]{1,0:T(8,128)(2,1)}, f32[8,128]{1,0:T(8,128)S(1)}) custom-call(s32[6]{0:T(128)S(1)} %stack.31.place_ref, bf16[768,512]{1,0:T(8,128)(2,1)S(1)} %get-tuple-element.149.refs_3_.refs_0_, bf16[768,512]{1,0:T(8,128)(2,1)S(1)} %get-tuple-element.175.refs_1_, ...), custom_call_target="tpu_custom_call", output_to_operand_aliasing={{0}: (5, {})} | custom-call | tf_op jit(solution)/shard_map/pallas_call | solution.py:45
  238.4 0.8 shard_map.115
  239.2 1.6 collective-permute-start.26
  240.8 1.5 collective-permute-start.27
  242.3 5.5 %shard_map.116 = (bf16[3072,3072]{1,0:T(8,128)(2,1)}, f32[8,128]{1,0:T(8,128)S(1)}) custom-call(s32[6]{0:T(128)S(1)} %stack.31.place_ref, bf16[768,512]{1,0:T(8,128)(2,1)S(1)} %get-tuple-element.149.refs_3_.refs_0_, bf16[768,512]{1,0:T(8,128)(2,1)S(1)} %get-tuple-element.175.refs_1_, ...), custom_call_target="tpu_custom_call", output_to_operand_aliasing={{0}: (5, {})} | custom-call | tf_op jit(solution)/shard_map/pallas_call | solution.py:45
  247.9 1.2 collective-permute-done.27.refs_3_
  249.1 1.5 shard_map.117
  (100 shorter events, 10.2 us)
Async XLA Ops:
  0.6 22.1 %slice-start = ((s8[4718592]{0:T(1024)(128)(4,1)}), s8[524288]{0:T(1024)(128)(4,1)S(1)}, s32[]{:S(2)}) async-start(s8[4718592]{0:T(1024)(128)(4,1)} %bitcast.6), calls=%async_computation | async-start | bytes 1048576
  0.8 1.3 copy-start.2
  2.6 14.2 %collective-permute-start.1 = (bf16[192,1024]{1,0:T(8,128)(2,1)S(1)}, bf16[192,1024]{1,0:T(8,128)(2,1)S(1)}, u32[]{:S(2)}, u32[]{:S(2)}) collective-permute-start(bf16[192,1024]{1,0:T(8,128)(2,1)S(1)} %get-tuple-element.101.refs_0_), channel_id=1, source_target_pairs={{0,1},{1,0},{2,3},{3,2},{4,5},{5,4},{6,7},{7,6},{8,9},{9,8},{10,11... | collective-permute-start | bytes 1179656 | tf_op jit(solution)/shard_map/ppermute | solution.py:415
  5.7 25.0 %collective-permute-start.3 = (bf16[192,1024]{1,0:T(8,128)(2,1)S(1)}, bf16[192,1024]{1,0:T(8,128)(2,1)S(1)}, u32[]{:S(2)}, u32[]{:S(2)}) collective-permute-start(bf16[192,1024]{1,0:T(8,128)(2,1)S(1)} %get-tuple-element.101.refs_0_), channel_id=1, source_target_pairs={{1,2},{2,1},{5,6},{6,5},{9,10},{10,9},{13,14},{14,13},{17,18},{18,... | collective-permute-start | bytes 1179656 | tf_op jit(solution)/shard_map/ppermute | solution.py:415
  6.3 2.3 copy-start
  8.6 14.1 %slice-start.1 = ((s8[4718592]{0:T(1024)(128)(4,1)}), s8[4194304]{0:T(1024)(128)(4,1)S(1)}, s32[]{:S(2)}) async-start(s8[4718592]{0:T(1024)(128)(4,1)} %bitcast.6), calls=%async_computation.1 | async-start | bytes 8388608
  16.8 50.9 %copy-start.10 = (bf16[768,512]{1,0:T(8,128)(2,1)}, bf16[768,512]{1,0:T(8,128)(2,1)S(1)}, u32[]{:S(2)}) copy-start(bf16[768,512]{1,0:T(8,128)(2,1)S(1)} %get-tuple-element.100.refs_0_) | copy-start | bytes 2359300
  16.8 48.8 %copy-start.3 = (bf16[192,3072]{1,0:T(8,128)(2,1)S(1)}, bf16[192,3072]{1,0:T(8,128)(2,1)}, u32[]{:S(2)}) copy-start(bf16[192,3072]{1,0:T(8,128)(2,1)} %refs_0_.18) | copy-start | bytes 3538948
  17.5 13.2 %collective-permute-start.2 = (bf16[192,1024]{1,0:T(8,128)(2,1)S(1)}, bf16[192,1024]{1,0:T(8,128)(2,1)S(1)}, u32[]{:S(2)}, u32[]{:S(2)}) collective-permute-start(bf16[192,1024]{1,0:T(8,128)(2,1)S(1)} %get-tuple-element.103), channel_id=1, source_target_pairs={{1,2},{2,1},{5,6},{6,5},{9,10},{10,9},{13,14},{14,13},{17,18},{18,... | collective-permute-start | bytes 1179656 | tf_op jit(solution)/shard_map/ppermute | solution.py:415
  18.1 13.3 %collective-permute-start.4 = (bf16[192,1024]{1,0:T(8,128)(2,1)S(1)}, bf16[192,1024]{1,0:T(8,128)(2,1)S(1)}, u32[]{:S(2)}, u32[]{:S(2)}) collective-permute-start(bf16[192,1024]{1,0:T(8,128)(2,1)S(1)} %get-tuple-element.107.refs_0_), channel_id=1, source_target_pairs={{0,1},{1,0},{2,3},{3,2},{4,5},{5,4},{6,7},{7,6},{8,9},{9,8},{10,11... | collective-permute-start | bytes 1179656 | tf_op jit(solution)/shard_map/ppermute | solution.py:415
  20.8 26.4 %collective-permute-start = (bf16[768,512]{1,0:T(8,128)(2,1)S(1)}, bf16[768,512]{1,0:T(8,128)(2,1)S(1)}, u32[]{:S(2)}, u32[]{:S(2)}) collective-permute-start(bf16[768,512]{1,0:T(8,128)(2,1)S(1)} %get-tuple-element.99.refs_0_), channel_id=1, source_target_pairs={{0,1},{3,2},{4,5},{7,6},{8,9},{11,10},{12,13},{15,14},{16,17},{19,... | collective-permute-start | bytes 2359304 | tf_op jit(solution)/shard_map/ppermute | solution.py:415
  30.7 64.1 %copy-start.6 = (bf16[768,512]{1,0:T(8,128)(2,1)}, bf16[768,512]{1,0:T(8,128)(2,1)S(1)}, u32[]{:S(2)}) copy-start(bf16[768,512]{1,0:T(8,128)(2,1)S(1)} %get-tuple-element.115.refs_0_) | copy-start | bytes 2359300
  30.7 74.8 %copy-start.4 = (bf16[768,512]{1,0:T(8,128)(2,1)}, bf16[768,512]{1,0:T(8,128)(2,1)S(1)}, u32[]{:S(2)}) copy-start(bf16[768,512]{1,0:T(8,128)(2,1)S(1)} %get-tuple-element.113.refs_5_.refs_0_) | copy-start | bytes 2359300
  32.1 15.9 %collective-permute-start.7 = (bf16[768,512]{1,0:T(8,128)(2,1)S(1)}, bf16[768,512]{1,0:T(8,128)(2,1)S(1)}, u32[]{:S(2)}, u32[]{:S(2)}) collective-permute-start(bf16[768,512]{1,0:T(8,128)(2,1)S(1)} %get-tuple-element.116.refs_3_.refs_0_), channel_id=1, source_target_pairs={{1,2},{2,1},{5,6},{6,5},{9,10},{10,9},{13,14},{14,13},{17,18},{18,... | collective-permute-start | bytes 2359304 | tf_op jit(solution)/shard_map/ppermute | solution.py:415
  32.9 31.2 %collective-permute-start.6 = (bf16[768,512]{1,0:T(8,128)(2,1)S(1)}, bf16[768,512]{1,0:T(8,128)(2,1)S(1)}, u32[]{:S(2)}, u32[]{:S(2)}) collective-permute-start(bf16[768,512]{1,0:T(8,128)(2,1)S(1)} %get-tuple-element.114), channel_id=1, source_target_pairs={{0,1},{1,0},{2,3},{3,2},{4,5},{5,4},{6,7},{7,6},{8,9},{9,8},{10,11... | collective-permute-start | bytes 2359304 | tf_op jit(solution)/shard_map/ppermute | solution.py:415
  48.0 18.3 %collective-permute-start.5 = (bf16[768,512]{1,0:T(8,128)(2,1)S(1)}, bf16[768,512]{1,0:T(8,128)(2,1)S(1)}, u32[]{:S(2)}, u32[]{:S(2)}) collective-permute-start(bf16[768,512]{1,0:T(8,128)(2,1)S(1)} %get-tuple-element.111), channel_id=1, source_target_pairs={{1,2},{2,1},{5,6},{6,5},{9,10},{10,9},{13,14},{14,13},{17,18},{18,... | collective-permute-start | bytes 2359304 | tf_op jit(solution)/shard_map/ppermute | solution.py:415
  48.8 32.2 %collective-permute-start.10 = (bf16[768,512]{1,0:T(8,128)(2,1)S(1)}, bf16[768,512]{1,0:T(8,128)(2,1)S(1)}, u32[]{:S(2)}, u32[]{:S(2)}) collective-permute-start(bf16[768,512]{1,0:T(8,128)(2,1)S(1)} %get-tuple-element.123), channel_id=1, source_target_pairs={{0,1},{1,0},{2,3},{3,2},{4,5},{5,4},{6,7},{7,6},{8,9},{9,8},{10,11... | collective-permute-start | bytes 2359304 | tf_op jit(solution)/shard_map/ppermute | solution.py:415
  66.2 34.1 %collective-permute-start.9 = (bf16[768,512]{1,0:T(8,128)(2,1)}, bf16[768,512]{1,0:T(8,128)(2,1)S(1)}, u32[]{:S(2)}, u32[]{:S(2)}) collective-permute-start(bf16[768,512]{1,0:T(8,128)(2,1)} %get-tuple-element.122), channel_id=1, source_target_pairs={{1,2},{2,1},{5,6},{6,5},{9,10},{10,9},{13,14},{14,13},{17,18},{18,... | collective-permute-start | bytes 2359304 | tf_op jit(solution)/shard_map/ppermute | solution.py:415
  67.8 37.7 %collective-permute-start.8 = (bf16[768,512]{1,0:T(8,128)(2,1)}, bf16[768,512]{1,0:T(8,128)(2,1)S(1)}, u32[]{:S(2)}, u32[]{:S(2)}) collective-permute-start(bf16[768,512]{1,0:T(8,128)(2,1)} %get-tuple-element.121.refs_1_), channel_id=1, source_target_pairs={{0,1},{1,0},{2,3},{3,2},{4,5},{5,4},{6,7},{7,6},{8,9},{9,8},{10,11... | collective-permute-start | bytes 2359304 | tf_op jit(solution)/shard_map/ppermute | solution.py:415
  82.5 36.2 %collective-permute-start.12 = (bf16[768,512]{1,0:T(8,128)(2,1)}, bf16[768,512]{1,0:T(8,128)(2,1)}, u32[]{:S(2)}, u32[]{:S(2)}) collective-permute-start(bf16[768,512]{1,0:T(8,128)(2,1)} %get-tuple-element.130), channel_id=1, source_target_pairs={{1,2},{2,1},{5,6},{6,5},{9,10},{10,9},{13,14},{14,13},{17,18},{18,... | collective-permute-start | bytes 2359304 | tf_op jit(solution)/shard_map/ppermute | solution.py:415
  82.5 29.3 %collective-permute-start.13 = (bf16[192,1024]{1,0:T(8,128)(2,1)S(1)}, bf16[192,1024]{1,0:T(8,128)(2,1)S(1)}, u32[]{:S(2)}, u32[]{:S(2)}) collective-permute-start(bf16[192,1024]{1,0:T(8,128)(2,1)S(1)} %get-tuple-element.132.refs_0_), channel_id=1, source_target_pairs={{0,1},{1,0},{2,3},{3,2},{4,5},{5,4},{6,7},{7,6},{8,9},{9,8},{10,11... | collective-permute-start | bytes 1179656 | tf_op jit(solution)/shard_map/ppermute | solution.py:415
  94.8 27.7 %copy-start.12 = (bf16[768,512]{1,0:T(8,128)(2,1)}, bf16[768,512]{1,0:T(8,128)(2,1)S(1)}, u32[]{:S(2)}) copy-start(bf16[768,512]{1,0:T(8,128)(2,1)S(1)} %get-tuple-element.126.refs_5_.refs_0_) | copy-start | bytes 2359300
  94.8 46.0 %copy-start.8 = (bf16[768,512]{1,0:T(8,128)(2,1)}, bf16[768,512]{1,0:T(8,128)(2,1)S(1)}, u32[]{:S(2)}) copy-start(bf16[768,512]{1,0:T(8,128)(2,1)S(1)} %get-tuple-element.131.refs_5_.refs_0_) | copy-start | bytes 2359300
  94.8 17.8 %slice-start.2 = ((s8[4718592]{0:T(1024)(128)(4,1)}), s8[4194304]{0:T(1024)(128)(4,1)S(1)}, s32[]{:S(2)}) async-start(s8[4718592]{0:T(1024)(128)(4,1)} %bitcast.8), calls=%async_computation.2 | async-start | bytes 8388608
  100.3 0.9 copy-start.24
  101.2 1.1 copy-start.11
  102.3 1.1 copy-start.25
  103.5 15.2 %copy-start.7 = (bf16[768,512]{1,0:T(8,128)(2,1)S(1)}, bf16[768,512]{1,0:T(8,128)(2,1)}, u32[]{:S(2)}) copy-start(bf16[768,512]{1,0:T(8,128)(2,1)} %copy-done.6) | copy-start | bytes 2359300
  104.1 19.7 %copy-start.14 = (bf16[768,512]{1,0:T(8,128)(2,1)}, bf16[768,512]{1,0:T(8,128)(2,1)S(1)}, u32[]{:S(2)}) copy-start(bf16[768,512]{1,0:T(8,128)(2,1)S(1)} %get-tuple-element.129.refs_1_.refs_3_) | copy-start | bytes 2359300
  104.1 18.4 %collective-permute-start.11 = (bf16[768,512]{1,0:T(8,128)(2,1)S(1)}, bf16[768,512]{1,0:T(8,128)(2,1)S(1)}, u32[]{:S(2)}, u32[]{:S(2)}) collective-permute-start(bf16[768,512]{1,0:T(8,128)(2,1)S(1)} %get-tuple-element.129.refs_1_.refs_3_), channel_id=1, source_target_pairs={{0,1},{1,0},{2,3},{3,2},{4,5},{5,4},{6,7},{7,6},{8,9},{9,8},{10,11... | collective-permute-start | bytes 2359304 | tf_op jit(solution)/shard_map/ppermute | solution.py:415
  106.3 28.1 %collective-permute-start.15 = (bf16[768,512]{1,0:T(8,128)(2,1)S(1)}, bf16[768,512]{1,0:T(8,128)(2,1)S(1)}, u32[]{:S(2)}, u32[]{:S(2)}) collective-permute-start(bf16[768,512]{1,0:T(8,128)(2,1)S(1)} %get-tuple-element.140), channel_id=1, source_target_pairs={{1,2},{2,1},{5,6},{6,5},{9,10},{10,9},{13,14},{14,13},{17,18},{18,... | collective-permute-start | bytes 2359304 | tf_op jit(solution)/shard_map/ppermute | solution.py:415
  106.3 6.3 %slice-start.3 = ((s8[4718592]{0:T(1024)(128)(4,1)}), s8[524288]{0:T(1024)(128)(4,1)S(1)}, s32[]{:S(2)}) async-start(s8[4718592]{0:T(1024)(128)(4,1)} %bitcast.8), calls=%async_computation.3 | async-start | bytes 1048576
  120.4 22.0 %copy-start.16 = (bf16[768,512]{1,0:T(8,128)(2,1)}, bf16[768,512]{1,0:T(8,128)(2,1)S(1)}, u32[]{:S(2)}) copy-start(bf16[768,512]{1,0:T(8,128)(2,1)S(1)} %get-tuple-element.139.refs_1_.refs_5_) | copy-start | bytes 2359300
  120.4 20.4 %collective-permute-start.14 = (bf16[768,512]{1,0:T(8,128)(2,1)S(1)}, bf16[768,512]{1,0:T(8,128)(2,1)S(1)}, u32[]{:S(2)}, u32[]{:S(2)}) collective-permute-start(bf16[768,512]{1,0:T(8,128)(2,1)S(1)} %get-tuple-element.139.refs_1_.refs_5_), channel_id=1, source_target_pairs={{0,1},{1,0},{2,3},{3,2},{4,5},{5,4},{6,7},{7,6},{8,9},{9,8},{10,11... | collective-permute-start | bytes 2359304 | tf_op jit(solution)/shard_map/ppermute | solution.py:415
  122.5 30.4 %collective-permute-start.18 = (bf16[768,512]{1,0:T(8,128)(2,1)S(1)}, bf16[768,512]{1,0:T(8,128)(2,1)S(1)}, u32[]{:S(2)}, u32[]{:S(2)}) collective-permute-start(bf16[768,512]{1,0:T(8,128)(2,1)S(1)} %get-tuple-element.149.refs_3_.refs_0_), channel_id=1, source_target_pairs={{1,2},{2,1},{5,6},{6,5},{9,10},{10,9},{13,14},{14,13},{17,18},{18,... | collective-permute-start | bytes 2359304 | tf_op jit(solution)/shard_map/ppermute | solution.py:415
  123.3 29.6 %collective-permute-start.17 = (bf16[768,512]{1,0:T(8,128)(2,1)S(1)}, bf16[768,512]{1,0:T(8,128)(2,1)S(1)}, u32[]{:S(2)}, u32[]{:S(2)}) collective-permute-start(bf16[768,512]{1,0:T(8,128)(2,1)S(1)} %get-tuple-element.148), channel_id=1, source_target_pairs={{1,2},{2,1},{5,6},{6,5},{9,10},{10,9},{13,14},{14,13},{17,18},{18,... | collective-permute-start | bytes 2359304 | tf_op jit(solution)/shard_map/ppermute | solution.py:415
  128.8 5.5 %copy-start.5 = (bf16[768,512]{1,0:T(8,128)(2,1)S(1)}, bf16[768,512]{1,0:T(8,128)(2,1)}, u32[]{:S(2)}) copy-start(bf16[768,512]{1,0:T(8,128)(2,1)} %copy-done.4) | copy-start | bytes 2359300
  135.0 17.9 %copy-start.18 = (bf16[768,512]{1,0:T(8,128)(2,1)}, bf16[768,512]{1,0:T(8,128)(2,1)S(1)}, u32[]{:S(2)}) copy-start(bf16[768,512]{1,0:T(8,128)(2,1)S(1)} %get-tuple-element.147.refs_7_.refs_1_) | copy-start | bytes 2359300
  135.0 26.8 %collective-permute-start.16 = (bf16[768,512]{1,0:T(8,128)(2,1)S(1)}, bf16[768,512]{1,0:T(8,128)(2,1)S(1)}, u32[]{:S(2)}, u32[]{:S(2)}) collective-permute-start(bf16[768,512]{1,0:T(8,128)(2,1)S(1)} %get-tuple-element.147.refs_7_.refs_1_), channel_id=1, source_target_pairs={{0,1},{1,0},{2,3},{3,2},{4,5},{5,4},{6,7},{7,6},{8,9},{9,8},{10,11... | collective-permute-start | bytes 2359304 | tf_op jit(solution)/shard_map/ppermute | solution.py:415
  142.4 36.5 %collective-permute-start.20 = (bf16[768,512]{1,0:T(8,128)(2,1)}, bf16[768,512]{1,0:T(8,128)(2,1)}, u32[]{:S(2)}, u32[]{:S(2)}) collective-permute-start(bf16[768,512]{1,0:T(8,128)(2,1)} %get-tuple-element.159), channel_id=1, source_target_pairs={{1,2},{2,1},{5,6},{6,5},{9,10},{10,9},{13,14},{14,13},{17,18},{18,... | collective-permute-start | bytes 2359304 | tf_op jit(solution)/shard_map/ppermute | solution.py:415
  147.4 5.5 %copy-start.13 = (bf16[768,512]{1,0:T(8,128)(2,1)S(1)}, bf16[768,512]{1,0:T(8,128)(2,1)}, u32[]{:S(2)}) copy-start(bf16[768,512]{1,0:T(8,128)(2,1)} %copy-done.12) | copy-start | bytes 2359300
  147.4 14.4 %copy-start.15 = (bf16[768,512]{1,0:T(8,128)(2,1)S(1)}, bf16[768,512]{1,0:T(8,128)(2,1)}, u32[]{:S(2)}) copy-start(bf16[768,512]{1,0:T(8,128)(2,1)} %copy-done.14) | copy-start | bytes 2359300
  147.4 14.4 %copy-start.17 = (bf16[768,512]{1,0:T(8,128)(2,1)S(1)}, bf16[768,512]{1,0:T(8,128)(2,1)}, u32[]{:S(2)}) copy-start(bf16[768,512]{1,0:T(8,128)(2,1)} %copy-done.16) | copy-start | bytes 2359300
  152.9 26.0 %copy-start.9 = (bf16[768,512]{1,0:T(8,128)(2,1)S(1)}, bf16[768,512]{1,0:T(8,128)(2,1)}, u32[]{:S(2)}) copy-start(bf16[768,512]{1,0:T(8,128)(2,1)} %copy-done.8) | copy-start | bytes 2359300
  153.6 34.0 %copy-start.20 = (bf16[768,512]{1,0:T(8,128)(2,1)}, bf16[768,512]{1,0:T(8,128)(2,1)S(1)}, u32[]{:S(2)}) copy-start(bf16[768,512]{1,0:T(8,128)(2,1)S(1)} %get-tuple-element.158.refs_1_.refs_2_) | copy-start | bytes 2359300
  153.6 34.0 %collective-permute-start.19 = (bf16[768,512]{1,0:T(8,128)(2,1)S(1)}, bf16[768,512]{1,0:T(8,128)(2,1)S(1)}, u32[]{:S(2)}, u32[]{:S(2)}) collective-permute-start(bf16[768,512]{1,0:T(8,128)(2,1)S(1)} %get-tuple-element.158.refs_1_.refs_2_), channel_id=1, source_target_pairs={{0,1},{1,0},{2,3},{3,2},{4,5},{5,4},{6,7},{7,6},{8,9},{9,8},{10,11... | collective-permute-start | bytes 2359304 | tf_op jit(solution)/shard_map/ppermute | solution.py:415
  161.8 1.1 copy-start.19
  180.6 17.8 %collective-permute-start.21 = (bf16[768,512]{1,0:T(8,128)(2,1)S(1)}, bf16[768,512]{1,0:T(8,128)(2,1)S(1)}, u32[]{:S(2)}, u32[]{:S(2)}) collective-permute-start(bf16[768,512]{1,0:T(8,128)(2,1)S(1)} %get-tuple-element.161.refs_4_.refs_1_), channel_id=1, source_target_pairs={{0,1},{1,0},{2,3},{3,2},{4,5},{5,4},{6,7},{7,6},{8,9},{9,8},{10,11... | collective-permute-start | bytes 2359304 | tf_op jit(solution)/shard_map/ppermute | solution.py:415
  187.6 10.8 %copy-start.22 = (bf16[768,512]{1,0:T(8,128)(2,1)}, bf16[768,512]{1,0:T(8,128)(2,1)S(1)}, u32[]{:S(2)}) copy-start(bf16[768,512]{1,0:T(8,128)(2,1)S(1)} %collective-permute-done.19.refs_2_.refs_3_) | copy-start | bytes 2359300
  198.4 1.1 copy-start.21
  199.5 1.1 copy-start.23
  211.5 1.4 copy-start.26
  212.9 4.7 %collective-permute-start.22 = (bf16[384,3072]{1,0:T(8,128)(2,1)}, bf16[384,3072]{1,0:T(8,128)(2,1)S(1)}, u32[]{:S(2)}, u32[]{:S(2)}) collective-permute-start(bf16[384,3072]{1,0:T(8,128)(2,1)} %copy-done.26), channel_id=1, source_target_pairs={{0,4},{4,0},{8,12},{12,8},{16,20},{20,16},{24,28},{28,24},{1,5},{5... | collective-permute-start | bytes 7077896 | tf_op jit(solution)/shard_map/ppermute | solution.py:419
  212.9 20.0 %collective-permute-start.25 = (bf16[768,512]{1,0:T(8,128)(2,1)S(1)}, bf16[768,512]{1,0:T(8,128)(2,1)S(1)}, u32[]{:S(2)}, u32[]{:S(2)}) collective-permute-start(bf16[768,512]{1,0:T(8,128)(2,1)S(1)} %get-tuple-element.175.refs_1_), channel_id=1, source_target_pairs={{0,1},{1,0},{2,3},{3,2},{4,5},{5,4},{6,7},{7,6},{8,9},{9,8},{10,11... | collective-permute-start | bytes 2359304 | tf_op jit(solution)/shard_map/ppermute | solution.py:415
  219.2 19.2 %collective-permute-start.23 = (bf16[192,1536]{1,0:T(8,128)(2,1)S(1)}, bf16[192,1536]{1,0:T(8,128)(2,1)S(1)}, u32[]{:S(2)}, u32[]{:S(2)}) collective-permute-start(bf16[192,1536]{1,0:T(8,128)(2,1)S(1)} %get-tuple-element.172), channel_id=1, source_target_pairs={{0,8},{4,12},{8,0},{12,4},{16,24},{20,28},{24,16},{28,20},{1,9},{5... | collective-permute-start | bytes 1769480 | tf_op jit(solution)/shard_map/ppermute | solution.py:419
  220.7 17.6 %collective-permute-start.24 = (bf16[192,1536]{1,0:T(8,128)(2,1)S(1)}, bf16[192,1536]{1,0:T(8,128)(2,1)S(1)}, u32[]{:S(2)}, u32[]{:S(2)}) collective-permute-start(bf16[192,1536]{1,0:T(8,128)(2,1)S(1)} %get-tuple-element.174), channel_id=1, source_target_pairs={{0,16},{4,20},{8,24},{12,28},{16,0},{20,4},{24,8},{28,12},{1,17},{... | collective-permute-start | bytes 1769480 | tf_op jit(solution)/shard_map/ppermute | solution.py:419
  222.2 2.3 copy-start.1
  239.2 8.7 %collective-permute-start.26 = (bf16[96,1536]{1,0:T(8,128)(2,1)S(1)}, bf16[96,1536]{1,0:T(8,128)(2,1)S(1)}, u32[]{:S(2)}, u32[]{:S(2)}) collective-permute-start(bf16[96,1536]{1,0:T(8,128)(2,1)S(1)} %get-tuple-element.182), channel_id=1, source_target_pairs={{0,16},{4,20},{8,24},{12,28},{16,0},{20,4},{24,8},{28,12},{1,17},{... | collective-permute-start | bytes 884744 | tf_op jit(solution)/shard_map/ppermute | solution.py:419
  240.8 8.4 %collective-permute-start.27 = (bf16[96,1536]{1,0:T(8,128)(2,1)S(1)}, bf16[96,1536]{1,0:T(8,128)(2,1)S(1)}, u32[]{:S(2)}, u32[]{:S(2)}) collective-permute-start(bf16[96,1536]{1,0:T(8,128)(2,1)S(1)} %get-tuple-element.184), channel_id=1, source_target_pairs={{0,8},{4,12},{8,0},{12,4},{16,24},{20,28},{24,16},{28,20},{1,9},{5... | collective-permute-start | bytes 884744 | tf_op jit(solution)/shard_map/ppermute | solution.py:419
